TPU v7x, 32 devices: a whole 2x2x4 slice. The times are simulated.
32 devices in a mesh: ta: 4 (over z), ha: 4 (over x, core), wa: 2 (over y).
Axes of the slice: x: 2, y: 2, z: 4, core: 2. Of those that a mesh axis runs over, the one named last changes fastest.
Arguments:
- clip: bfloat16 [8, 16, 32, 256], P('ta', 'ha', 'wa'), may hold values from -6 to 6
- conv_weight: bfloat16 [6912, 256], replicated, may hold values from -0.078125 to 0.078125
- down_weight: bfloat16 [6912, 256], replicated, may hold values from -0.078125 to 0.078125
- out_cotangent: bfloat16 [4, 8, 16, 256], P('ta', 'ha', 'wa'), may hold values from -6 to 6
Outputs:
- grad_clip: bfloat16 [8, 16, 32, 256], P('ta', 'ha', 'wa')
- grad_conv: float32 [6912, 256], P(('ha', 'wa'), 'ta')
- grad_down: float32 [6912, 256], P(('ha', 'wa'), 'ta')
All inputs are finite; a program needn't handle non-finite values.
Results may differ from a plain program's by a relative error of at most 0.014.
Values may be sent and summed in bfloat16 or wider, within the bound.
A program may use at most 64 MiB of HBM per device.

v0:
```python
import jax
import jax.numpy as jnp
from jax import lax
from jax.sharding import PartitionSpec as P


def from_behind(x, axis, by):
    count = lax.axis_size(axis)
    pairs = [(i, i + by) for i in range(count) if 0 <= i + by < count]
    return lax.ppermute(x, axis, pairs)


def padded(block, sides, width):
    for axis, dim in sides:
        count = lax.axis_size(axis)
        forward = [(i, i + 1) for i in range(count - 1)]
        backward = [(target, source) for source, target in forward]
        low = lax.ppermute(
            lax.slice_in_dim(block, block.shape[dim] - width, None, axis=dim), axis, forward
        )
        high = lax.ppermute(lax.slice_in_dim(block, 0, width, axis=dim), axis, backward)
        block = jnp.concatenate([low, block, high], axis=dim)
    return block


def extend_past(values):
    earlier = from_behind(values[-2:], "ta", 1)
    return jnp.concatenate([earlier, values], axis=0)


def extend_next(values, frames):
    later = from_behind(values[:frames], "ta", -1)
    return jnp.concatenate([values, later], axis=0)


def with_rims(values):
    return padded(values, (("ha", 1), ("wa", 2)), 1)


def convolve(inputs, kernel, specs, padding, lhs_step, rhs_step):
    return lax.conv_general_dilated(
        inputs,
        kernel,
        (1, 1, 1),
        padding,
        lhs_dilation=lhs_step,
        rhs_dilation=rhs_step,
        dimension_numbers=specs,
        preferred_element_type=jnp.float32,
    )


def local(clip, conv_weight, down_weight, out_cotangent):
    channels = clip.shape[-1]
    share = channels // lax.axis_size("ta")
    first_kernel = conv_weight.reshape(3, 3, 3, channels, channels)
    down_kernel = down_weight.reshape(3, 3, 3, channels, channels)
    coarse_t, coarse_h, coarse_w = (
        out_cotangent.shape[0],
        out_cotangent.shape[1],
        out_cotangent.shape[2],
    )
    unit = (1, 1, 1)
    valid = [(0, 0), (0, 0), (0, 0)]
    forward_specs = ("NDHWC", "DHWIO", "NDHWC")
    back_specs = ("NDHWC", "DHWOI", "NDHWC")
    weight_specs = ("CDHWN", "IDHWO", "DHWNC")
    padded_clip = with_rims(extend_past(clip))
    pre_act = convolve(padded_clip[None], first_kernel, forward_specs, valid, unit, unit)[0]
    activation = jax.nn.silu(pre_act).astype(jnp.bfloat16)
    padded_act = with_rims(extend_past(activation))
    act_window = padded_act[: 2 * coarse_t + 1, : 2 * coarse_h + 1, : 2 * coarse_w + 1]
    clip_blocks, act_blocks = (
        lax.all_gather(padded_clip[None], "ta", axis=0, tiled=True),
        lax.all_gather(act_window[None], "ta", axis=0, tiled=True),
    )
    coarse_ext = with_rims(extend_next(out_cotangent, 1))[:, 1:, 1:]
    flipped_down = down_kernel[::-1, ::-1, ::-1]
    grad_act = convolve(
        coarse_ext[None], flipped_down, back_specs, [(0, 1), (1, 0), (1, 0)], (2, 2, 2), unit
    )[0]
    sigma = jax.nn.sigmoid(pre_act)
    grad_pre = (grad_act * sigma * (1.0 + pre_act * (1.0 - sigma))).astype(jnp.bfloat16)
    padded_grad = with_rims(extend_next(grad_pre, 2))
    flipped_first = first_kernel[::-1, ::-1, ::-1]
    grad_clip = convolve(padded_grad[None], flipped_first, back_specs, valid, unit, unit)[0].astype(
        jnp.bfloat16
    )
    start = lax.axis_index("ta") * share
    cot_all = lax.all_gather(out_cotangent[None], "ta", axis=0, tiled=True)
    grad_all = lax.all_gather(grad_pre[None], "ta", axis=0, tiled=True)
    cot_blocks = lax.dynamic_slice_in_dim(cot_all, start, share, 4)
    grad_blocks = lax.dynamic_slice_in_dim(grad_all, start, share, 4)
    grad_down = convolve(act_blocks, cot_blocks, weight_specs, valid, unit, (2, 2, 2))
    grad_conv = convolve(clip_blocks, grad_blocks, weight_specs, valid, unit, unit)
    terms = (grad_conv.reshape(27 * channels, share), grad_down.reshape(27 * channels, share))
    totals = (
        lax.psum_scatter(terms[0], ("ha", "wa"), scatter_dimension=0, tiled=True),
        lax.psum_scatter(terms[1], ("ha", "wa"), scatter_dimension=0, tiled=True),
    )
    return (grad_clip, totals[0], totals[1])


def solution(mesh):
    return jax.shard_map(
        local,
        mesh=mesh,
        in_specs=(P("ta", "ha", "wa", None), P(), P(), P("ta", "ha", "wa", None)),
        out_specs=(P("ta", "ha", "wa", None), P(("ha", "wa"), "ta"), P(("ha", "wa"), "ta")),
        check_vma=False,
    )
```

profile of v0, /device:TPU:0, one launch (start us, length us, event | category | flops | bytes accessed | tf_op | source)
XLA Modules:
  0.0 196.2 jit_solution(1469553798861798159)
XLA Ops:
  7.2 5.8 %collective-permute-start.4 = (bf16[2,4,16,256]{3,2,1,0:T(8,128)(2,1)}, bf16[2,4,16,256]{3,2,1,0:T(8,128)(2,1)}, u32[]{:S(2)}, u32[]{:S(2)}) collective-permute-start(bf16[2,4,16,256]{3,2,1,0:T(8,128)(2,1)} %param.4), channel_id=1, source_target_pairs={{0,8},{8,16},{16,24},{1,9},{9,17},{17,25},{2,10},{10,18},{18,26},{... | collective-permute-start | bytes 196616 | tf_op jit(solution)/shard_map/ppermute | solution.py:10
  15.0 3.9 %collective-permute-done = bf16[1,2,8,256]{3,2,1,0:T(8,128)(2,1)} collective-permute-done((bf16[1,2,8,256]{3,2,1,0:T(8,128)(2,1)}, bf16[1,2,8,256]{3,2,1,0:T(8,128)(2,1)}, u32[]{:S(2)}, u32[]{:S(2)}) %collective-permute-start) | collective-permute-done | bytes 8224 | tf_op jit(solution)/shard_map/ppermute | solution.py:10
  20.9 3.0 %collective-permute-start.1 = (bf16[2,1,8,256]{3,2,1,0:T(8,128)(2,1)S(1)}, bf16[2,1,8,256]{3,2,1,0:T(8,128)(2,1)S(1)}, u32[]{:S(2)}, u32[]{:S(2)}) collective-permute-start(bf16[2,1,8,256]{3,2,1,0:T(8,128)(2,1)S(1)} %get-tuple-element.28), channel_id=1, source_target_pairs={{0,2},{2,4},{4,6},{1,3},{3,5},{5,7},{8,10},{10,12},{12,14},{9,11},... | collective-permute-start | bytes 24584 | tf_op jit(solution)/shard_map/ppermute | solution.py:18
  26.9 3.6 %collective-permute-start.5 = (bf16[4,1,16,256]{3,2,1,0:T(8,128)(2,1)S(1)}, bf16[4,1,16,256]{3,2,1,0:T(8,128)(2,1)S(1)}, u32[]{:S(2)}, u32[]{:S(2)}) collective-permute-start(bf16[4,1,16,256]{3,2,1,0:T(8,128)(2,1)S(1)} %get-tuple-element.26), channel_id=1, source_target_pairs={{0,2},{2,4},{4,6},{1,3},{3,5},{5,7},{8,10},{10,12},{12,14},{9,11},... | collective-permute-start | bytes 98312 | tf_op jit(solution)/shard_map/ppermute | solution.py:18
  33.3 4.6 %collective-permute-start.7 = (bf16[4,6,1,256]{3,2,1,0:T(2,128)(2,1)S(1)}, bf16[4,6,1,256]{3,2,1,0:T(2,128)(2,1)S(1)}, u32[]{:S(2)}, u32[]{:S(2)}) collective-permute-start(bf16[4,6,1,256]{3,2,1,0:T(2,128)(2,1)S(1)} %get-tuple-element.18), channel_id=1, source_target_pairs={{0,1},{2,3},{4,5},{6,7},{8,9},{10,11},{12,13},{14,15},{16,17},{18,... | collective-permute-start | bytes 36872 | tf_op jit(solution)/shard_map/ppermute | solution.py:18
  39.9 1.6 add_divide_fusion
  41.7 24.1 %all-gather = bf16[16,6,18,256]{3,2,1,0:T(8,128)(2,1)S(1)} all-gather(bf16[4,6,18,256]{3,2,1,0:T(8,128)(2,1)S(1)} %get-tuple-element.12), channel_id=2, replica_groups=mesh['ta'=4,'ha'=4,'wa'=2] {'ta'}, dimensions={0}, use_global_device_ids=true | all-gather | bytes 1105920 | tf_op jit(solution)/shard_map/all_gather | solution.py:74
  65.8 2.0 %fusion.23 = (bf16[1,2,4,16,256]{4,0,3,2,1:T(2,128)(2,1)S(1)}, f32[1,2,4,16,256]{4,0,3,2,1:T(1,128)}) fusion(f32[2,4,1,16,256]{4,1,3,0,2:T(4,128)S(1)} %slice.81, f32[2,4,1,16,256]{4,1,3,0,2:T(4,128)S(1)} %slice.80, bf16[3,3,3,256,256]{4,3,2,1,0:T(8,128)(2,1)S(1)} %bitcast.72, bf16[1,2,3,9,256]{4,3,2,1,0:T(8,128)(2,1)S(1)} %fusion.29), kind=kOutput, calls=%fused_computation.33 | convolution fusion | flops 56721408 | bytes 4025344 | tf_op jit(solution)/shard_map/conv_general_dilated | solution.py:41
  67.8 14.3 %all_gather.13 = bf16[4,2,4,16,256]{4,3,2,1,0:T(8,128)(2,1)S(1)} all-gather(bf16[1,2,4,16,256]{4,3,2,1,0:T(8,128)(2,1)S(1)} %copy.75), channel_id=1, replica_groups=mesh['ta'=4,'ha'=4,'wa'=2] {'ta'}, dimensions={0}, use_global_device_ids=true | all-gather | bytes 327680 | tf_op jit(solution)/shard_map/all_gather | solution.py:91
  82.2 5.3 %fusion.3 = f32[3,3,3,256,64]{4,3,2,1,0:T(8,128)} fusion(bf16[4,4,6,18,256]{4,3,2,1,0:T(8,128)(2,1)S(1)} %bitcast.64, bf16[4,2,4,16,64]{4,3,2,1,0:T(8,128)(2,1)S(1)} %constant_dynamic-slice_fusion.1), kind=kOutput, calls=%fused_computation.6 | convolution fusion | flops 452984832 | bytes 2719744
  88.6 1.6 multiply_convert_fusion
  91.5 1.9 collective-permute-done.14
  94.7 3.0 %collective-permute-start.15 = (bf16[4,1,16,256]{3,2,1,0:T(8,128)(2,1)S(1)}, bf16[4,1,16,256]{3,2,1,0:T(8,128)(2,1)S(1)}, u32[]{:S(2)}, u32[]{:S(2)}) collective-permute-start(bf16[4,1,16,256]{3,2,1,0:T(8,128)(2,1)S(1)} %get-tuple-element.20), channel_id=1, source_target_pairs={{0,2},{2,4},{4,6},{1,3},{3,5},{5,7},{8,10},{10,12},{12,14},{9,11},... | collective-permute-start | bytes 98312 | tf_op jit(solution)/shard_map/ppermute | solution.py:18
  97.8 14.4 %all-gather.2 = bf16[4,2,8,256]{3,2,1,0:T(8,128)(2,1)S(1)} all-gather(bf16[1,2,8,256]{3,2,1,0:T(8,128)(2,1)S(1)} %copy-done.1), channel_id=4, replica_groups=mesh['ta'=4,'ha'=4,'wa'=2] {'ta'}, dimensions={0}, use_global_device_ids=true | all-gather | bytes 40960 | tf_op jit(solution)/shard_map/all_gather | solution.py:90
  112.2 4.1 %collective-permute-start.17 = (bf16[4,6,1,256]{3,2,1,0:T(2,128)(2,1)S(1)}, bf16[4,6,1,256]{3,2,1,0:T(2,128)(2,1)S(1)}, u32[]{:S(2)}, u32[]{:S(2)}) collective-permute-start(bf16[4,6,1,256]{3,2,1,0:T(2,128)(2,1)S(1)} %pad_maximum_fusion.12), channel_id=1, source_target_pairs={{0,1},{2,3},{4,5},{6,7},{8,9},{10,11},{12,13},{14,15},{16,17},{18,... | collective-permute-start | bytes 36872 | tf_op jit(solution)/shard_map/ppermute | solution.py:18
  116.4 1.7 collective-permute-done.17
  118.2 17.4 %all-gather.1 = bf16[12,5,17,256]{3,2,1,0:T(8,128)(2,1)S(1)} all-gather(bf16[3,5,17,256]{3,2,1,0:T(8,128)(2,1)S(1)} %pad_maximum_fusion.1), channel_id=3, replica_groups=mesh['ta'=4,'ha'=4,'wa'=2] {'ta'}, dimensions={0}, use_global_device_ids=true | all-gather | bytes 652800 | tf_op jit(solution)/shard_map/all_gather | solution.py:75
  135.6 2.7 %fusion.5 = f32[3,3,3,256,64]{4,3,2,1,0:T(8,128)} fusion(bf16[4,3,5,17,256]{4,3,2,1,0:T(8,128)(2,1)S(1)} %bitcast.67, bf16[4,2,8,64]{3,2,1,0:T(8,128)(2,1)S(1)} %constant_dynamic-slice_fusion), kind=kOutput, calls=%fused_computation.8 | convolution fusion | flops 56623104 | bytes 2299904
  139.7 5.1 %collective-permute-done.9 = bf16[2,4,16,256]{3,2,1,0:T(8,128)(2,1)S(1)} collective-permute-done((bf16[2,4,16,256]{3,2,1,0:T(8,128)(2,1)}, bf16[2,4,16,256]{3,2,1,0:T(8,128)(2,1)S(1)}, u32[]{:S(2)}, u32[]{:S(2)}) %collective-permute-start.9) | collective-permute-done | bytes 65568 | tf_op jit(solution)/shard_map/ppermute | solution.py:10
  146.8 3.0 %collective-permute-start.10 = (bf16[4,1,16,256]{3,2,1,0:T(8,128)(2,1)S(1)}, bf16[4,1,16,256]{3,2,1,0:T(8,128)(2,1)S(1)}, u32[]{:S(2)}, u32[]{:S(2)}) collective-permute-start(bf16[4,1,16,256]{3,2,1,0:T(8,128)(2,1)S(1)} %get-tuple-element.24), channel_id=1, source_target_pairs={{0,2},{2,4},{4,6},{1,3},{3,5},{5,7},{8,10},{10,12},{12,14},{9,11},... | collective-permute-start | bytes 98312 | tf_op jit(solution)/shard_map/ppermute | solution.py:18
  152.8 4.5 %collective-permute-start.12 = (bf16[4,6,1,256]{3,2,1,0:T(2,128)(2,1)S(1)}, bf16[4,6,1,256]{3,2,1,0:T(2,128)(2,1)S(1)}, u32[]{:S(2)}, u32[]{:S(2)}) collective-permute-start(bf16[4,6,1,256]{3,2,1,0:T(2,128)(2,1)S(1)} %get-tuple-element.16), channel_id=1, source_target_pairs={{0,1},{2,3},{4,5},{6,7},{8,9},{10,11},{12,13},{14,15},{16,17},{18,... | collective-permute-start | bytes 36872 | tf_op jit(solution)/shard_map/ppermute | solution.py:18
  162.2 1.9 copy.84
  164.1 23.3 %reduce-scatter.9.cloned.1.call-done = f32[864,64]{1,0:T(8,128)} async-done(((f32[6912,64]{1,0:T(8,128)}), f32[864,64]{1,0:T(8,128)}) %reduce-scatter.9.cloned.1.call-update) | async-done | bytes 221200
  187.5 1.9 copy.86
  (76 shorter events, 26.8 us)
Async XLA Ops:
  7.2 32.7 %copy-start = (bf16[6912,256]{1,0:T(8,128)(2,1)S(1)}, bf16[6912,256]{1,0:T(8,128)(2,1)}, u32[]{:S(2)}) copy-start(bf16[6912,256]{1,0:T(8,128)(2,1)} %param.5) | copy-start | bytes 10616836
  7.2 155.1 %reduce-scatter.7.cloned.1.call-start = ((), (), s32[]{:S(2)}) async-start(), calls=%async_computation.2 | async-start | bytes 3981312
  7.2 16.7 %collective-permute-start.4 = (bf16[2,4,16,256]{3,2,1,0:T(8,128)(2,1)}, bf16[2,4,16,256]{3,2,1,0:T(8,128)(2,1)}, u32[]{:S(2)}, u32[]{:S(2)}) collective-permute-start(bf16[2,4,16,256]{3,2,1,0:T(8,128)(2,1)} %param.4), channel_id=1, source_target_pairs={{0,8},{8,16},{16,24},{1,9},{9,17},{17,25},{2,10},{10,18},{18,26},{... | collective-permute-start | bytes 196616 | tf_op jit(solution)/shard_map/ppermute | solution.py:10
  13.0 5.9 %collective-permute-start = (bf16[1,2,8,256]{3,2,1,0:T(8,128)(2,1)}, bf16[1,2,8,256]{3,2,1,0:T(8,128)(2,1)}, u32[]{:S(2)}, u32[]{:S(2)}) collective-permute-start(bf16[1,2,8,256]{3,2,1,0:T(8,128)(2,1)} %param.7), channel_id=1, source_target_pairs={{8,0},{16,8},{24,16},{9,1},{17,9},{25,17},{10,2},{18,10},{26,18},{... | collective-permute-start | bytes 24584 | tf_op jit(solution)/shard_map/ppermute | solution.py:10
  15.0 24.8 %copy-start.3 = (pred[8,3]{0,1:T(4,128)(4,1)S(1)}, pred[8,3]{0,1:T(4,128)(4,1)}, u32[]{:S(2)}) copy-start(pred[8,3]{0,1:T(4,128)(4,1)} %constant.25) | copy-start | bytes 76
  19.6 11.0 %collective-permute-start.2 = (bf16[2,1,8,256]{3,2,1,0:T(8,128)(2,1)S(1)}, bf16[2,1,8,256]{3,2,1,0:T(8,128)(2,1)S(1)}, u32[]{:S(2)}, u32[]{:S(2)}) collective-permute-start(bf16[2,1,8,256]{3,2,1,0:T(8,128)(2,1)S(1)} %get-tuple-element.29), channel_id=1, source_target_pairs={{2,0},{4,2},{6,4},{3,1},{5,3},{7,5},{10,8},{12,10},{14,12},{11,9},... | collective-permute-start | bytes 24584 | tf_op jit(solution)/shard_map/ppermute | solution.py:21
  20.9 9.7 %collective-permute-start.1 = (bf16[2,1,8,256]{3,2,1,0:T(8,128)(2,1)S(1)}, bf16[2,1,8,256]{3,2,1,0:T(8,128)(2,1)S(1)}, u32[]{:S(2)}, u32[]{:S(2)}) collective-permute-start(bf16[2,1,8,256]{3,2,1,0:T(8,128)(2,1)S(1)} %get-tuple-element.28), channel_id=1, source_target_pairs={{0,2},{2,4},{4,6},{1,3},{3,5},{5,7},{8,10},{10,12},{12,14},{9,11},... | collective-permute-start | bytes 24584 | tf_op jit(solution)/shard_map/ppermute | solution.py:18
  25.6 6.3 %collective-permute-start.6 = (bf16[4,1,16,256]{3,2,1,0:T(8,128)(2,1)S(1)}, bf16[4,1,16,256]{3,2,1,0:T(8,128)(2,1)S(1)}, u32[]{:S(2)}, u32[]{:S(2)}) collective-permute-start(bf16[4,1,16,256]{3,2,1,0:T(8,128)(2,1)S(1)} %get-tuple-element.27), channel_id=1, source_target_pairs={{2,0},{4,2},{6,4},{3,1},{5,3},{7,5},{10,8},{12,10},{14,12},{11,9},... | collective-permute-start | bytes 98312 | tf_op jit(solution)/shard_map/ppermute | solution.py:21
  26.9 5.0 %collective-permute-start.5 = (bf16[4,1,16,256]{3,2,1,0:T(8,128)(2,1)S(1)}, bf16[4,1,16,256]{3,2,1,0:T(8,128)(2,1)S(1)}, u32[]{:S(2)}, u32[]{:S(2)}) collective-permute-start(bf16[4,1,16,256]{3,2,1,0:T(8,128)(2,1)S(1)} %get-tuple-element.26), channel_id=1, source_target_pairs={{0,2},{2,4},{4,6},{1,3},{3,5},{5,7},{8,10},{10,12},{12,14},{9,11},... | collective-permute-start | bytes 98312 | tf_op jit(solution)/shard_map/ppermute | solution.py:18
  30.6 7.2 %collective-permute-start.3 = (bf16[2,4,1,256]{3,2,1,0:T(2,128)(2,1)S(1)}, bf16[2,4,1,256]{3,2,1,0:T(2,128)(2,1)S(1)}, u32[]{:S(2)}, u32[]{:S(2)}) collective-permute-start(bf16[2,4,1,256]{3,2,1,0:T(2,128)(2,1)S(1)} %pad_maximum_fusion.22), channel_id=1, source_target_pairs={{1,0},{3,2},{5,4},{7,6},{9,8},{11,10},{13,12},{15,14},{17,16},{19,... | collective-permute-start | bytes 12296 | tf_op jit(solution)/shard_map/ppermute | solution.py:21
  32.0 5.9 %collective-permute-start.8 = (bf16[4,6,1,256]{3,2,1,0:T(2,128)(2,1)S(1)}, bf16[4,6,1,256]{3,2,1,0:T(2,128)(2,1)S(1)}, u32[]{:S(2)}, u32[]{:S(2)}) collective-permute-start(bf16[4,6,1,256]{3,2,1,0:T(2,128)(2,1)S(1)} %get-tuple-element.19), channel_id=1, source_target_pairs={{1,0},{3,2},{5,4},{7,6},{9,8},{11,10},{13,12},{15,14},{17,16},{19,... | collective-permute-start | bytes 36872 | tf_op jit(solution)/shard_map/ppermute | solution.py:21
  33.3 6.1 %collective-permute-start.7 = (bf16[4,6,1,256]{3,2,1,0:T(2,128)(2,1)S(1)}, bf16[4,6,1,256]{3,2,1,0:T(2,128)(2,1)S(1)}, u32[]{:S(2)}, u32[]{:S(2)}) collective-permute-start(bf16[4,6,1,256]{3,2,1,0:T(2,128)(2,1)S(1)} %get-tuple-element.18), channel_id=1, source_target_pairs={{0,1},{2,3},{4,5},{6,7},{8,9},{10,11},{12,13},{14,15},{16,17},{18,... | collective-permute-start | bytes 36872 | tf_op jit(solution)/shard_map/ppermute | solution.py:18
  39.9 25.9 %copy-start.2 = (bf16[6912,256]{1,0:T(8,128)(2,1)S(1)}, bf16[6912,256]{1,0:T(8,128)(2,1)}, u32[]{:S(2)}) copy-start(bf16[6912,256]{1,0:T(8,128)(2,1)} %param.6) | copy-start | bytes 10616836
  87.6 99.9 %reduce-scatter.9.cloned.1.call-start = ((), (), s32[]{:S(2)}) async-start(), calls=%async_computation.3 | async-start | bytes 3981312
  90.2 3.2 %collective-permute-start.14 = (bf16[2,4,16,256]{3,2,1,0:T(8,128)(2,1)S(1)}, bf16[2,4,16,256]{3,2,1,0:T(8,128)(2,1)S(1)}, u32[]{:S(2)}, u32[]{:S(2)}) collective-permute-start(bf16[2,4,16,256]{3,2,1,0:T(8,128)(2,1)S(1)} %get-tuple-element.22), channel_id=1, source_target_pairs={{0,8},{8,16},{16,24},{1,9},{9,17},{17,25},{2,10},{10,18},{18,26},{... | collective-permute-start | bytes 196616 | tf_op jit(solution)/shard_map/ppermute | solution.py:10
  93.4 18.7 %collective-permute-start.16 = (bf16[4,1,16,256]{3,2,1,0:T(8,128)(2,1)S(1)}, bf16[4,1,16,256]{3,2,1,0:T(8,128)(2,1)S(1)}, u32[]{:S(2)}, u32[]{:S(2)}) collective-permute-start(bf16[4,1,16,256]{3,2,1,0:T(8,128)(2,1)S(1)} %get-tuple-element.21), channel_id=1, source_target_pairs={{2,0},{4,2},{6,4},{3,1},{5,3},{7,5},{10,8},{12,10},{14,12},{11,9},... | collective-permute-start | bytes 98312 | tf_op jit(solution)/shard_map/ppermute | solution.py:21
  94.7 17.5 %collective-permute-start.15 = (bf16[4,1,16,256]{3,2,1,0:T(8,128)(2,1)S(1)}, bf16[4,1,16,256]{3,2,1,0:T(8,128)(2,1)S(1)}, u32[]{:S(2)}, u32[]{:S(2)}) collective-permute-start(bf16[4,1,16,256]{3,2,1,0:T(8,128)(2,1)S(1)} %get-tuple-element.20), channel_id=1, source_target_pairs={{0,2},{2,4},{4,6},{1,3},{3,5},{5,7},{8,10},{10,12},{12,14},{9,11},... | collective-permute-start | bytes 98312 | tf_op jit(solution)/shard_map/ppermute | solution.py:18
  112.2 6.0 %collective-permute-start.17 = (bf16[4,6,1,256]{3,2,1,0:T(2,128)(2,1)S(1)}, bf16[4,6,1,256]{3,2,1,0:T(2,128)(2,1)S(1)}, u32[]{:S(2)}, u32[]{:S(2)}) collective-permute-start(bf16[4,6,1,256]{3,2,1,0:T(2,128)(2,1)S(1)} %pad_maximum_fusion.12), channel_id=1, source_target_pairs={{0,1},{2,3},{4,5},{6,7},{8,9},{10,11},{12,13},{14,15},{16,17},{18,... | collective-permute-start | bytes 36872 | tf_op jit(solution)/shard_map/ppermute | solution.py:18
  138.4 21.8 %copy-start.4 = (pred[8,3]{0,1:T(4,128)(4,1)S(1)}, pred[8,3]{0,1:T(4,128)(4,1)}, u32[]{:S(2)}) copy-start(pred[8,3]{0,1:T(4,128)(4,1)} %constant.25) | copy-start | bytes 76
  138.4 6.4 %collective-permute-start.9 = (bf16[2,4,16,256]{3,2,1,0:T(8,128)(2,1)}, bf16[2,4,16,256]{3,2,1,0:T(8,128)(2,1)S(1)}, u32[]{:S(2)}, u32[]{:S(2)}) collective-permute-start(bf16[2,4,16,256]{3,2,1,0:T(8,128)(2,1)} %get-tuple-element.23), channel_id=1, source_target_pairs={{8,0},{16,8},{24,16},{9,1},{17,9},{25,17},{10,2},{18,10},{26,18},{... | collective-permute-start | bytes 196616 | tf_op jit(solution)/shard_map/ppermute | solution.py:10
  145.5 4.3 %collective-permute-start.11 = (bf16[4,1,16,256]{3,2,1,0:T(8,128)(2,1)S(1)}, bf16[4,1,16,256]{3,2,1,0:T(8,128)(2,1)S(1)}, u32[]{:S(2)}, u32[]{:S(2)}) collective-permute-start(bf16[4,1,16,256]{3,2,1,0:T(8,128)(2,1)S(1)} %get-tuple-element.25), channel_id=1, source_target_pairs={{2,0},{4,2},{6,4},{3,1},{5,3},{7,5},{10,8},{12,10},{14,12},{11,9},... | collective-permute-start | bytes 98312 | tf_op jit(solution)/shard_map/ppermute | solution.py:21
  146.8 3.9 %collective-permute-start.10 = (bf16[4,1,16,256]{3,2,1,0:T(8,128)(2,1)S(1)}, bf16[4,1,16,256]{3,2,1,0:T(8,128)(2,1)S(1)}, u32[]{:S(2)}, u32[]{:S(2)}) collective-permute-start(bf16[4,1,16,256]{3,2,1,0:T(8,128)(2,1)S(1)} %get-tuple-element.24), channel_id=1, source_target_pairs={{0,2},{2,4},{4,6},{1,3},{3,5},{5,7},{8,10},{10,12},{12,14},{9,11},... | collective-permute-start | bytes 98312 | tf_op jit(solution)/shard_map/ppermute | solution.py:18
  151.5 5.9 %collective-permute-start.13 = (bf16[4,6,1,256]{3,2,1,0:T(2,128)(2,1)S(1)}, bf16[4,6,1,256]{3,2,1,0:T(2,128)(2,1)S(1)}, u32[]{:S(2)}, u32[]{:S(2)}) collective-permute-start(bf16[4,6,1,256]{3,2,1,0:T(2,128)(2,1)S(1)} %get-tuple-element.17), channel_id=1, source_target_pairs={{1,0},{3,2},{5,4},{7,6},{9,8},{11,10},{13,12},{15,14},{17,16},{19,... | collective-permute-start | bytes 36872 | tf_op jit(solution)/shard_map/ppermute | solution.py:21
  152.8 6.1 %collective-permute-start.12 = (bf16[4,6,1,256]{3,2,1,0:T(2,128)(2,1)S(1)}, bf16[4,6,1,256]{3,2,1,0:T(2,128)(2,1)S(1)}, u32[]{:S(2)}, u32[]{:S(2)}) collective-permute-start(bf16[4,6,1,256]{3,2,1,0:T(2,128)(2,1)S(1)} %get-tuple-element.16), channel_id=1, source_target_pairs={{0,1},{2,3},{4,5},{6,7},{8,9},{10,11},{12,13},{14,15},{16,17},{18,... | collective-permute-start | bytes 36872 | tf_op jit(solution)/shard_map/ppermute | solution.py:18
  (1 other events, 10.2 us)
Sparse Core Ops, SparseCore 0:
  87.7 48.1 reduce-scatter.6
  139.3 48.0 reduce-scatter.8
where the time goes:
time: 197 us; the launch traced here: 196 us
  blocking collectives  70.2 us (36%)
  starting transfers between devices  44.7 us (23%)
  waiting for transfers between devices  39.7 us (20%)
  between operations  14.5 us (7%)
  matrix products  13 us (7%)
  local copies, waits for them, and re-layouts  9.59 us (5%)
  other arithmetic  4.5 us (2%)
    ppermute x7, starting transfers between devices, padded(): lax.ppermute(lax.slice_in_dim(block, block.shape[dim] - width, None, axis...  26 us
    all_gather x1, blocking collectives, local(): lax.all_gather(padded_clip[None], 'ta', axis=0, tiled=True)  24.1 us
    unnamed x4, waiting for transfers between devices  23.4 us
    all_gather x1, blocking collectives, local(): lax.all_gather(act_window[None], 'ta', axis=0, tiled=True)  17.4 us
    all_gather x1, blocking collectives, local(): cot_all = lax.all_gather(out_cotangent[None], 'ta', axis=0, tiled=True)  14.4 us
    all_gather x1, blocking collectives, local(): grad_all = lax.all_gather(grad_pre[None], 'ta', axis=0, tiled=True)  14.3 us
    ppermute x4, waiting for transfers between devices, from_behind(): return lax.ppermute(x, axis, pairs)  10.8 us
    ppermute x4, starting transfers between devices, from_behind(): return lax.ppermute(x, axis, pairs)  9.67 us
  transfers between devices with their start and end apart: 20, of which 8 were waited for; matrix products, arithmetic and copies ran while one was open for 8% of the time, Pallas kernels for 0%

commit v1 on v0

v1 whole, which is shorter than its diff:
```python
import functools

import jax
import jax.numpy as jnp
from jax import lax
from jax.experimental import pallas as pl
from jax.experimental.pallas import tpu as pltpu
from jax.sharding import PartitionSpec as P

MESH = pl.DeviceIdType.MESH
SIDES = [(dh, dw) for dh in (-1, 0, 1) for dw in (-1, 0, 1) if (dh, dw) != (0, 0)]


def gather_kernel(sizes, x_ref, mid, rows, cols, diag, zs, zr, ps, pr):
    n_t, n_h, n_w = sizes
    t, h, w = lax.axis_index("ta"), lax.axis_index("ha"), lax.axis_index("wa")

    def exists(dh, dw):
        return (h + dh >= 0) & (h + dh < n_h) & (w + dw >= 0) & (w + dw < n_w)

    def slot(s, dh, dw):
        if dw == 0:
            return rows.at[s, 0 if dh > 0 else 1]
        if dh == 0:
            return cols.at[s, 0 if dw > 0 else 1]
        return diag.at[s, 0 if dh > 0 else 1, 0 if dw > 0 else 1]

    def part(dh, dw):
        if dw == 0:
            return pl.ds(0, 6) if dh < 0 else pl.ds(5, 6)
        if dh == 0:
            return pl.ds(4, 3)
        return pl.ds(4, 2) if dh < 0 else pl.ds(5, 2)

    barrier = pltpu.get_barrier_semaphore()
    count = n_t - 1
    for d in range(1, n_t):
        pl.semaphore_signal(
            barrier, inc=1, device_id=(lax.rem(t + d, n_t), h, w), device_id_type=MESH
        )
    for dh, dw in SIDES:
        there = exists(dh, dw)
        count = count + jnp.where(there, 1, 0)

        @pl.when(there)
        def _():
            pl.semaphore_signal(
                barrier, inc=1, device_id=(t, h + dh, w + dw), device_id_type=MESH
            )

    pl.semaphore_wait(barrier, count)

    along = []
    for d in range(1, n_t):
        copy = pltpu.make_async_remote_copy(
            src_ref=x_ref,
            dst_ref=mid.at[t],
            send_sem=zs.at[d - 1],
            recv_sem=zr.at[d - 1],
            device_id=(lax.rem(t + d, n_t), h, w),
            device_id_type=MESH,
        )
        copy.start()
        along.append(copy)

    def beside(d, s, i):
        dh, dw = SIDES[i]
        source = x_ref if d == 0 else mid.at[s]
        return pltpu.make_async_remote_copy(
            src_ref=source.at[part(dh, dw)],
            dst_ref=slot(s, dh, dw),
            send_sem=ps.at[d, i],
            recv_sem=pr.at[d, i],
            device_id=(t, h + dh, w + dw),
            device_id_type=MESH,
        )

    for d in range(n_t):
        s = lax.rem(t - d + n_t, n_t)
        if d > 0:
            along[d - 1].wait_recv()
        for i, (dh, dw) in enumerate(SIDES):

            @pl.when(exists(dh, dw))
            def _():
                beside(d, s, i).start()

        if d == 0:
            mid[t] = x_ref[...]
            for i, (dh, dw) in enumerate(SIDES):

                @pl.when(jnp.logical_not(exists(-dh, -dw)))
                def _():
                    for block in range(n_t):
                        target = slot(block, dh, dw)
                        target[...] = jnp.zeros(target.shape, target.dtype)

    for d in range(n_t):
        s = lax.rem(t - d + n_t, n_t)
        if d > 0:
            along[d - 1].wait_send()
        for i, (dh, dw) in enumerate(SIDES):

            @pl.when(exists(dh, dw))
            def _():
                beside(d, s, i).wait_send()

            @pl.when(exists(-dh, -dw))
            def _():
                beside(d, s, i).wait_recv()


def gather(x, sizes):
    n_t = sizes[0]
    tile = x.shape[1:]
    vmem = pl.BlockSpec(memory_space=pltpu.VMEM)
    shapes = [(n_t, 11), (n_t, 2, 6), (n_t, 2, 3), (n_t, 2, 2, 2)]
    return pl.pallas_call(
        functools.partial(gather_kernel, sizes),
        out_shape=[jax.ShapeDtypeStruct(shape + tile, x.dtype) for shape in shapes],
        in_specs=[vmem],
        out_specs=[vmem] * 4,
        scratch_shapes=[
            pltpu.SemaphoreType.DMA((n_t - 1,)),
            pltpu.SemaphoreType.DMA((n_t - 1,)),
            pltpu.SemaphoreType.DMA((n_t, 8)),
            pltpu.SemaphoreType.DMA((n_t, 8)),
        ],
        compiler_params=pltpu.CompilerParams(
            collective_id=0, has_side_effects=True, vmem_limit_bytes=32 * 2**20
        ),
    )(x)


def reduce_kernel(sizes, x_ref, out, pair, own, got, pair_sems, ss, rs):
    n_x, n_w = sizes
    t, h, w = lax.axis_index("ta"), lax.axis_index("ha"), lax.axis_index("wa")
    x, core = h // 2, lax.rem(h, 2)
    chips = n_x * n_w
    me = x * n_w + w

    def place(d):
        chip = lax.rem(me + d, chips)
        return (t, (chip // n_w) * 2 + core, lax.rem(chip, n_w))

    barrier = pltpu.get_barrier_semaphore()
    other = (t, h + 1 - 2 * core, w)
    pl.semaphore_signal(barrier, inc=1, device_id=other, device_id_type=MESH)
    for d in range(1, chips):
        pl.semaphore_signal(barrier, inc=1, device_id=place(d), device_id_type=MESH)
    pl.semaphore_wait(barrier, chips)

    def swap(d):
        chip = lax.rem(me + d, chips)
        return pltpu.make_async_remote_copy(
            src_ref=x_ref.at[chip // n_w, 1 - core, lax.rem(chip, n_w)],
            dst_ref=pair.at[chip],
            send_sem=pair_sems.at[0, d],
            recv_sem=pair_sems.at[1, d],
            device_id=other,
            device_id_type=MESH,
        )

    def send(d):
        return pltpu.make_async_remote_copy(
            src_ref=own.at[d],
            dst_ref=got.at[d],
            send_sem=ss.at[d],
            recv_sem=rs.at[d],
            device_id=place(d),
            device_id_type=MESH,
        )

    order = list(range(1, chips)) + [0]
    for d in order:
        swap(d).start()
    for d in order:
        chip = lax.rem(me + d, chips)
        swap(d).wait_recv()
        mine = x_ref[chip // n_w, core, lax.rem(chip, n_w)].astype(jnp.float32)
        both = mine + pair[chip].astype(jnp.float32)
        if d > 0:
            own[d] = both.astype(own.dtype)
            send(d).start()
        else:
            out[...] = both
    for d in range(1, chips):
        send(d).wait_recv()
        out[...] += got[d].astype(jnp.float32)
    for d in range(chips):
        swap(d).wait_send()
        if d > 0:
            send(d).wait_send()


def reduce_scatter(x, sizes):
    n_x, n_w = sizes
    chips = n_x * n_w
    share = x.shape[3:]
    vmem = pl.BlockSpec(memory_space=pltpu.VMEM)
    return pl.pallas_call(
        functools.partial(reduce_kernel, sizes),
        out_shape=jax.ShapeDtypeStruct(share, jnp.float32),
        in_specs=[vmem],
        out_specs=vmem,
        scratch_shapes=[
            pltpu.VMEM((chips,) + share, x.dtype),
            pltpu.VMEM((chips,) + share, x.dtype),
            pltpu.VMEM((chips,) + share, x.dtype),
            pltpu.SemaphoreType.DMA((2, chips)),
            pltpu.SemaphoreType.DMA((chips,)),
            pltpu.SemaphoreType.DMA((chips,)),
        ],
        compiler_params=pltpu.CompilerParams(
            collective_id=1, has_side_effects=True, vmem_limit_bytes=32 * 2**20
        ),
    )(x)


def convolve(inputs, kernel, specs, padding, lhs_step, rhs_step):
    return lax.conv_general_dilated(
        inputs,
        kernel,
        (1, 1, 1),
        padding,
        lhs_dilation=lhs_step,
        rhs_dilation=rhs_step,
        dimension_numbers=specs,
        preferred_element_type=jnp.float32,
    )


def local(clip, conv_weight, down_weight, out_cotangent):
    channels = clip.shape[-1]
    n_t, n_h, n_w = (lax.axis_size(axis) for axis in ("ta", "ha", "wa"))
    t, h, w = lax.axis_index("ta"), lax.axis_index("ha"), lax.axis_index("wa")
    share = channels // n_t
    first_kernel = conv_weight.reshape(3, 3, 3, channels, channels)
    down_kernel = down_weight.reshape(3, 3, 3, channels, channels)
    unit = (1, 1, 1)
    valid = [(0, 0), (0, 0), (0, 0)]
    forward_specs = ("NDHWC", "DHWIO", "NDHWC")
    back_specs = ("NDHWC", "DHWOI", "NDHWC")
    weight_specs = ("CDHWN", "IDHWO", "DHWNC")

    edges = jnp.concatenate([clip[:, :, :2], clip[:, :, -2:]], axis=2)
    packed = jnp.concatenate(
        [
            clip[:, :2].reshape(4, 16, channels),
            edges[:, :2].reshape(1, 16, channels),
            out_cotangent.reshape(1, 16, channels),
            edges[:, 2:].reshape(1, 16, channels),
            clip[:, 2:].reshape(4, 16, channels),
        ],
        axis=0,
    )
    mid, rows, cols, diag = gather(packed, (n_t, n_h, n_w))
    frames = 2 * n_t

    def half(chunk):
        return chunk.reshape(frames, 2, 16, channels)

    def edge(chunk):
        return chunk.reshape(frames, 2, 4, channels)

    def coarse(chunk):
        return chunk.reshape(n_t, 2, 8, channels)

    centre = jnp.concatenate(
        [half(rows[:, 0, 2:6]), half(mid[:, 0:4]), half(mid[:, 7:11]), half(rows[:, 1, 0:4])],
        axis=1,
    )
    left, right = (
        jnp.concatenate(
            [
                edge(diag[:, 0, side, 1]),
                edge(cols[:, side, 0]),
                edge(cols[:, side, 2]),
                edge(diag[:, 1, side, 0]),
            ],
            axis=1,
        )
        for side in (0, 1)
    )
    clip_ext = jnp.concatenate([left[:, :, 2:], centre, right[:, :, :2]], axis=2)
    cot_rows = [
        jnp.concatenate([coarse(a), coarse(b), coarse(c)], axis=2)
        for a, b, c in (
            (diag[:, 0, 0, 0], rows[:, 0, 0], diag[:, 0, 1, 0]),
            (cols[:, 0, 1], mid[:, 5], cols[:, 1, 1]),
            (diag[:, 1, 0, 1], rows[:, 1, 5], diag[:, 1, 1, 1]),
        )
    ]
    cot_ext = jnp.concatenate(cot_rows, axis=1)[:, 1:5, 7:17]
    cot_mid = coarse(mid[:, 5])

    row = lax.broadcasted_iota(jnp.int32, (1, 6, 18, 1), 1) + (h * 4 - 1)
    col = lax.broadcasted_iota(jnp.int32, (1, 6, 18, 1), 2) + (w * 16 - 1)
    inside = (row >= 0) & (row < 4 * n_h) & (col >= 0) & (col < 16 * n_w)
    pre_act = convolve(
        clip_ext[None], first_kernel, forward_specs, [(2, 0), (0, 0), (0, 0)], unit, unit
    )[0]
    grad_act = convolve(
        cot_ext[None],
        down_kernel[::-1, ::-1, ::-1],
        back_specs,
        [(0, 3), (0, 1), (0, 1)],
        (2, 2, 2),
        unit,
    )[0]
    sigma = jax.nn.sigmoid(pre_act)
    activation = jnp.where(inside, pre_act * sigma, 0.0).astype(jnp.bfloat16)
    grad_pre = jnp.where(
        inside, grad_act * sigma * (1.0 + pre_act * (1.0 - sigma)), 0.0
    ).astype(jnp.bfloat16)

    start = t * share

    def blocks(values, depth):
        ahead = jnp.pad(values, ((2, 0), (0, 0), (0, 0), (0, 0)))
        return jnp.stack([ahead[2 * i : 2 * i + depth] for i in range(n_t)])

    act_blocks = blocks(activation[:, :5, :17], 3)
    clip_blocks = blocks(clip_ext[:, 1:7, 1:19], 4)
    cot_blocks = lax.dynamic_slice_in_dim(cot_mid, start, share, 3)[:, None]
    grad_mid = lax.dynamic_slice_in_dim(grad_pre[:, 1:5, 1:17], start, share, 3)
    grad_blocks = grad_mid.reshape(n_t, 2, 4, 16, share)
    grad_down = convolve(act_blocks, cot_blocks, weight_specs, valid, unit, (2, 2, 2))
    grad_conv = convolve(clip_blocks, grad_blocks, weight_specs, valid, unit, unit)
    terms = jnp.concatenate(
        [grad_conv.reshape(27 * channels, share), grad_down.reshape(27 * channels, share)], axis=1
    ).astype(jnp.bfloat16)
    terms = terms.reshape(n_h // 2, 2, n_w, 27 * channels // (n_h * n_w), 2 * share)
    total = reduce_scatter(terms, (n_h // 2, n_w))

    later = jnp.pad(grad_pre, ((0, 2), (0, 0), (0, 0), (0, 0)))
    grad_ext = lax.dynamic_slice_in_dim(later, 2 * t, 4, 0)
    grad_clip = convolve(
        grad_ext[None], first_kernel[::-1, ::-1, ::-1], back_specs, valid, unit, unit
    )[0].astype(jnp.bfloat16)
    return (grad_clip, total[:, :share], total[:, share:])


def solution(mesh):
    return jax.shard_map(
        local,
        mesh=mesh,
        in_specs=(P("ta", "ha", "wa", None), P(), P(), P("ta", "ha", "wa", None)),
        out_specs=(P("ta", "ha", "wa", None), P(("ha", "wa"), "ta"), P(("ha", "wa"), "ta")),
        check_vma=False,
    )
```

time: 197 us -> 127 us (0.64)
  blocking collectives: 70.2 us -> 0 us
  starting transfers between devices: 44.7 us -> 0 us
  local copies, waits for them, and re-layouts: 9.59 us -> 53.6 us
  waiting for transfers between devices: 39.7 us -> 0 us
  Pallas kernels: 0 us -> 32.6 us
  matrix products: 13 us -> 29.1 us
  between operations: 14.5 us -> 0.98 us
  other arithmetic: 4.5 us -> 8.41 us
    all_gather x4 -> x0, blocking collectives: 70.2 us -> none  [the longest x1 24.1 us: local(): lax.all_gather(padded_clip[None], 'ta', axis=0, tiled=True)]
    ppermute x18 -> x0, starting transfers between devices: 44.7 us -> none  [the longest x7 26 us: padded(): lax.ppermute(lax.slice_in_dim(block, block.shape[dim] - width, None, axis...]
    another operation x0 -> x34, local copies, waits for them, and re-layouts: none -> 34.5 us  [the longest x16 21.6 us: edge(): return chunk.reshape(frames, 2, 4, channels)]
    pallas_call x0 -> x2, Pallas kernels: none -> 32.6 us  [the longest x1 17.5 us: gather(): pl.pallas_call(functools.partial(gather_kernel, sizes), out_shape=[jax.Sh...]
    conv_general_dilated x3 -> x5, matrix products: 4.9 us -> 29.1 us  [convolve(): lax.conv_general_dilated(inputs, kernel, (1, 1, 1), padding, lhs_dilation...]
    unnamed x4 -> x0, waiting for transfers between devices: 23.4 us -> none
    ppermute x18 -> x0, waiting for transfers between devices: 16.4 us -> none  [the longest x4 10.8 us: from_behind(): return lax.ppermute(x, axis, pairs)]
    unnamed x2 -> x0, matrix products: 8.07 us -> none
  transfers between devices with their start and end apart: 20 -> 0, of which waited for: 8 -> 0; matrix products, arithmetic and copies ran while one was open for 8% -> 0% of each run, Pallas kernels for 0% -> 0%
where the time goes in v1:
time: 127 us; the launch traced here: 125 us
  local copies, waits for them, and re-layouts  53.6 us (42%)
  Pallas kernels  32.6 us (26%)
  matrix products  29.1 us (23%)
  other arithmetic  8.41 us (7%)
    conv_general_dilated x5, matrix products, convolve(): lax.conv_general_dilated(inputs, kernel, (1, 1, 1), padding, lhs_dilation...  29.1 us
    another operation x16, local copies, waits for them, and re-layouts, edge(): return chunk.reshape(frames, 2, 4, channels)  21.6 us
    pallas_call x1, Pallas kernels, gather(): pl.pallas_call(functools.partial(gather_kernel, sizes), out_shape=[jax.Sh...  17.5 us
    pallas_call x1, Pallas kernels, reduce_scatter(): pl.pallas_call(functools.partial(reduce_kernel, sizes), out_shape=jax.Sha...  15.1 us
    unnamed x31, local copies, waits for them, and re-layouts  8.62 us
    another operation x2, local copies, waits for them, and re-layouts  5.13 us
    another operation x12, local copies, waits for them, and re-layouts, blocks(): return jnp.stack([ahead[2 * i:2 * i + depth] for i in range(n_t)])  4.77 us
    concatenate x1, other arithmetic, local(): jnp.concatenate([grad_conv.reshape(27 * channels, share), grad_down.resha...  2.98 us

profile of v1, /device:TPU:0, one launch (start us, length us, event | category | flops | bytes accessed | tf_op | source)
XLA Modules:
  0.0 124.7 jit_solution(2122634666467815631)
XLA Ops:
  0.7 2.0 %copy-done = bf16[6912,256]{1,0:T(8,128)(2,1)S(1)} copy-done((bf16[6912,256]{1,0:T(8,128)(2,1)S(1)}, bf16[6912,256]{1,0:T(8,128)(2,1)}, u32[]{:S(2)}) %copy-start) | copy-done | bytes 3538968
  6.9 17.5 %shard_map.67 = (bf16[4,11,16,256]{3,2,1,0:T(8,128)(2,1)S(1)}, bf16[4,2,6,16,256]{4,3,2,1,0:T(8,128)(2,1)S(1)}, bf16[4,2,3,16,256]{4,3,2,1,0:T(8,128)(2,1)S(1)}, bf16[4,2,2,2,16,256]{5,4,3,2,1,0:T(8,128)(2,1)S(1)}) custom-call(bf16[11,16,256]{2,1,0:T(8,128)(2,1)S(1)} %constant_dynamic-update-slice_fusion.x_ref), custom_call_target="tpu_custom_call" | custom-call | tf_op jit(solution)/shard_map/pallas_call | solution.py:118
  32.8 1.4 %reshape_squeeze.76 = bf16[8,2,4,256]{3,2,1,0:T(4,128)(2,1)} reshape(bf16[4,1,1,1,16,256]{5,4,3,2,1,0:T(8,128)(2,1)} %get-tuple-element.46) | data formatting | bytes 65536 | tf_op jit(solution)/shard_map/reshape;squeeze | solution.py:264
  34.2 1.4 %copy.140 = bf16[8,2,4,256]{3,1,2,0:T(2,128)(2,1)} copy(bf16[8,2,4,256]{3,2,1,0:T(4,128)(2,1)} %reshape_squeeze.76) | data formatting | bytes 65536 | tf_op jit(solution)/shard_map/reshape;squeeze | solution.py:264
  35.5 1.4 %reshape_squeeze.73 = bf16[8,2,4,256]{3,2,1,0:T(4,128)(2,1)} reshape(bf16[4,1,1,1,16,256]{5,4,3,2,1,0:T(8,128)(2,1)} %get-tuple-element.47) | data formatting | bytes 65536 | tf_op jit(solution)/shard_map/reshape;squeeze | solution.py:264
  36.9 1.4 %copy.137 = bf16[8,2,4,256]{3,1,2,0:T(2,128)(2,1)} copy(bf16[8,2,4,256]{3,2,1,0:T(4,128)(2,1)} %reshape_squeeze.73) | data formatting | bytes 65536 | tf_op jit(solution)/shard_map/reshape;squeeze | solution.py:264
  38.3 1.4 %reshape_squeeze.70 = bf16[8,2,4,256]{3,2,1,0:T(4,128)(2,1)} reshape(bf16[4,1,1,1,16,256]{5,4,3,2,1,0:T(8,128)(2,1)} %get-tuple-element.48) | data formatting | bytes 65536 | tf_op jit(solution)/shard_map/reshape;squeeze | solution.py:264
  39.7 1.4 %copy.132 = bf16[8,2,4,256]{3,1,2,0:T(2,128)(2,1)} copy(bf16[8,2,4,256]{3,2,1,0:T(4,128)(2,1)} %reshape_squeeze.70) | data formatting | bytes 65536 | tf_op jit(solution)/shard_map/reshape;squeeze | solution.py:264
  44.4 1.5 %fusion.58 = (bf16[4,1,1,16,256]{4,3,2,1,0:T(8,128)(2,1)}, bf16[4,1,1,16,256]{4,3,2,1,0:T(8,128)(2,1)}, bf16[4,1,1,16,256]{4,3,2,1,0:T(8,128)(2,1)}, bf16[4,1,1,...) fusion(bf16[4,2,3,16,256]{4,3,2,1,0:T(8,128)(2,1)} %copy-done.3), kind=kLoop, calls=%fused_computation.110 | loop fusion | bytes 393216 | tf_op jit(solution)/shard_map/slice | solution.py:277
  45.8 1.5 %fusion.42 = bf16[1,4,4,10,256]{4,3,2,1,0:T(8,128)(2,1)} fusion(bf16[4,2,8,256]{3,2,1,0:T(8,128)(2,1)} %get-tuple-element.49, bf16[4,2,8,256]{3,2,1,0:T(8,128)(2,1)S(1)} %get-tuple-element.42, bf16[4,2,8,256]{3,2,1,0:T(8,128)(2,1)} %get-tuple-element.50, bf16[4,2,8,256]{3,2,1,0:T(8,128)(2,1)S(1)} %get-tuple-element.57, ...), kind=kLoop, calls=%fused_computation.66 | loop fusion | flops 737280 | bytes 376832 | tf_op jit(solution)/shard_map/broadcast_in_dim | solution.py:304
  48.8 1.4 %copy.130 = bf16[8,2,4,256]{3,1,2,0:T(2,128)(2,1)} copy(bf16[8,2,4,256]{3,2,1,0:T(4,128)(2,1)} %reshape_squeeze.68) | data formatting | bytes 65536 | tf_op jit(solution)/shard_map/reshape;squeeze | solution.py:264
  54.3 1.4 %copy.138 = bf16[8,2,4,256]{3,1,2,0:T(2,128)(2,1)} copy(bf16[8,2,4,256]{3,2,1,0:T(4,128)(2,1)} %reshape_squeeze.74) | data formatting | bytes 65536 | tf_op jit(solution)/shard_map/reshape;squeeze | solution.py:264
  57.9 2.1 %fusion.20 = bf16[8,8,20,256]{3,1,2,0:T(8,128)(2,1)S(1)} fusion(bf16[8,2,4,256]{3,1,2,0:T(2,128)(2,1)} %copy.140, bf16[8,2,4,256]{3,1,2,0:T(2,128)(2,1)} %copy.139, bf16[8,2,4,256]{3,1,2,0:T(2,128)(2,1)} %copy.138, bf16[8,2,4,256]{3,1,2,0:T(2,128)(2,1)} %copy.137, bf16[8,2,4,256]{3,1,2,0:T(2,128)(2,1)} %copy.132, bf16[8,2,4,256]{3,1,2,0:T(2,128)(2,1)S(1)} %copy.131, ...), kind=kLoop, calls=%fused_computation.33 | loop fusion | flops 7864320 | bytes 1441792 | tf_op jit(solution)/shard_map/concatenate | solution.py:285
  61.3 4.3 %fusion.39 = f32[1,8,6,18,256]{4,0,3,2,1:T(1,128)S(1)} fusion(bf16[3,3,3,256,256]{4,3,2,1,0:T(8,128)(2,1)S(1)} %bitcast.124, bf16[1,4,4,10,256]{4,3,2,1,0:T(8,128)(2,1)S(1)} %copy-done.8), kind=kOutput, calls=%fused_computation.62 | convolution fusion | flops 318504960 | bytes 4505600 | tf_op jit(solution)/shard_map/conv_general_dilated | solution.py:221
  65.7 16.2 %fusion = f32[1,8,6,18,256]{4,0,3,2,1:T(1,128)S(1)} fusion(bf16[3,3,3,256,256]{4,3,2,1,0:T(8,128)(2,1)S(1)} %bitcast.110, bf16[1,8,8,20,256]{4,2,3,1,0:T(8,128)(2,1)S(1)} %bitcast.114), kind=kOutput, calls=%fused_computation.3 | convolution fusion | flops 2675441664 | bytes 5079040 | tf_op jit(solution)/shard_map/conv_general_dilated | solution.py:221
  86.9 2.6 %convolution_convert_fusion = bf16[3,3,3,256,64]{3,4,2,1,0:T(8,128)(2,1)} fusion(bf16[1,3,5,17,256]{4,0,3,2,1:T(2,128)(2,1)S(1)} %copy.164, bf16[1,3,5,17,256]{4,0,3,2,1:T(2,128)(2,1)S(1)} %copy.163, bf16[1,3,5,17,256]{4,0,3,2,1:T(2,128)(2,1)S(1)} %copy.162, bf16[1,3,5,17,256]{4,0,3,2,1:T(2,128)(2,1)S(1)} %copy.161, ...), kind=kOutput, calls=%fused_computation.1 | convolution fusion | flops 59154432 | bytes 1415168 | tf_op jit(solution)/shard_map/conv_general_dilated | solution.py:221
  89.5 2.6 %copy.166 = bf16[3,3,3,256,64]{4,3,2,1,0:T(8,128)(2,1)} copy(bf16[3,3,3,256,64]{3,4,2,1,0:T(8,128)(2,1)} %convolution_convert_fusion) | data formatting | bytes 1769472 | tf_op jit(solution)/shard_map/convert.2
  92.0 1.4 %slice_bitcast_fusion.2 = (bf16[1,4,6,18,256]{4,2,3,1,0:T(8,128)(2,1)S(1)}, bf16[1,4,6,18,256]{4,2,3,1,0:T(8,128)(2,1)S(1)}, bf16[1,4,6,18,256]{4,2,3,1,0:T(8,128)(2,1)S(1)}) fusion(bf16[8,8,20,256]{3,1,2,0:T(8,128)(2,1)} %copy-done.4), kind=kLoop, calls=%fused_computation.55 | loop fusion | bytes 1327104 | tf_op jit(solution)/shard_map/stack | solution.py:321
  94.5 4.7 %convolution_convert_fusion.1 = bf16[3,3,3,256,64]{3,4,2,1,0:T(8,128)(2,1)} fusion(bf16[1,4,6,18,256]{4,0,3,2,1:T(2,128)(2,1)S(1)} %copy.153, bf16[1,4,6,18,256]{4,0,3,2,1:T(2,128)(2,1)S(1)} %copy.152, bf16[1,4,6,18,256]{4,0,3,2,1:T(2,128)(2,1)S(1)} %copy.151, bf16[1,4,6,18,256]{4,0,3,2,1:T(2,128)(2,1)S(1)} %copy-done.5, ...), kind=kOutput, calls=%fused_computation.2 | convolution fusion | flops 456966144 | bytes 1835008 | tf_op jit(solution)/shard_map/conv_general_dilated | solution.py:221
  99.2 2.6 %copy.156 = bf16[3,3,3,256,64]{4,3,2,1,0:T(8,128)(2,1)} copy(bf16[3,3,3,256,64]{3,4,2,1,0:T(8,128)(2,1)} %convolution_convert_fusion.1) | data formatting | bytes 1769472 | tf_op jit(solution)/shard_map/convert.3
  101.8 3.0 %pad_maximum_fusion.x_ref = bf16[2,2,2,864,128]{4,3,2,1,0:T(8,128)(2,1)S(1)} fusion(bf16[2,2,2,864,64]{4,3,2,1,0:T(8,128)(2,1)} %bitcast.112, bf16[2,2,2,864,64]{4,3,2,1,0:T(8,128)(2,1)} %bitcast.113), kind=kLoop, calls=%fused_computation | loop fusion | flops 3538944 | bytes 3538944 | tf_op jit(solution)/shard_map/concatenate | solution.py:330
  104.8 15.1 %shard_map.68 = f32[864,128]{1,0:T(8,128)S(1)} custom-call(bf16[2,2,2,864,128]{4,3,2,1,0:T(8,128)(2,1)S(1)} %pad_maximum_fusion.x_ref), custom_call_target="tpu_custom_call" | custom-call | tf_op jit(solution)/shard_map/pallas_call | solution.py:201
  120.9 1.9 %copy.169 = f32[864,64]{0,1:T(8,128)} copy(f32[864,64]{1,0:T(8,128)} %get-tuple-element.34) | data formatting | bytes 442368
  122.8 1.9 %copy.168 = f32[864,64]{0,1:T(8,128)} copy(f32[864,64]{1,0:T(8,128)} %get-tuple-element.35) | data formatting | bytes 442368
  (79 shorter events, 31.8 us)
Async XLA Ops:
  0.6 2.0 %copy-start = (bf16[6912,256]{1,0:T(8,128)(2,1)S(1)}, bf16[6912,256]{1,0:T(8,128)(2,1)}, u32[]{:S(2)}) copy-start(bf16[6912,256]{1,0:T(8,128)(2,1)} %param.5) | copy-start | bytes 10616836
  24.4 0.7 copy-start.1
  25.2 0.7 copy-start.3
  25.8 0.8 copy-start.2
  30.2 2.5 %copy-start.6 = (bf16[4,2,8,256]{3,2,1,0:T(8,128)(2,1)}, bf16[4,2,8,256]{3,2,1,0:T(8,128)(2,1)S(1)}, u32[]{:S(2)}) copy-start(bf16[4,2,8,256]{3,2,1,0:T(8,128)(2,1)S(1)} %slice_bitcast_fusion.11) | copy-start | bytes 98308
  57.9 3.5 %copy-start.8 = (bf16[1,4,4,10,256]{4,3,2,1,0:T(8,128)(2,1)S(1)}, bf16[1,4,4,10,256]{4,3,2,1,0:T(8,128)(2,1)}, u32[]{:S(2)}) copy-start(bf16[1,4,4,10,256]{4,3,2,1,0:T(8,128)(2,1)} %fusion.42) | copy-start | bytes 245764
  57.9 3.4 %copy-start.10 = (bf16[6912,256]{1,0:T(8,128)(2,1)S(1)}, bf16[6912,256]{1,0:T(8,128)(2,1)}, u32[]{:S(2)}) copy-start(bf16[6912,256]{1,0:T(8,128)(2,1)} %param.6) | copy-start | bytes 10616836
  60.0 5.7 %copy-start.4 = (bf16[8,8,20,256]{3,1,2,0:T(8,128)(2,1)}, bf16[8,8,20,256]{3,1,2,0:T(8,128)(2,1)S(1)}, u32[]{:S(2)}) copy-start(bf16[8,8,20,256]{3,1,2,0:T(8,128)(2,1)S(1)} %fusion.20) | copy-start | bytes 1966084
  65.7 16.2 %copy-start.9 = (pred[6,18]{1,0:T(8,128)(4,1)S(1)}, pred[6,18]{1,0:T(8,128)(4,1)}, u32[]{:S(2)}) copy-start(pred[6,18]{1,0:T(8,128)(4,1)} %and_and_fusion) | copy-start | bytes 328
  82.4 1.2 copy-start.11
  92.0 2.5 %copy-start.5 = (bf16[1,4,6,18,256]{4,0,3,2,1:T(2,128)(2,1)S(1)}, bf16[1,4,6,18,256]{4,0,3,2,1:T(2,128)(2,1)}, u32[]{:S(2)}) copy-start(bf16[1,4,6,18,256]{4,0,3,2,1:T(2,128)(2,1)} %copy.150) | copy-start | bytes 663556
  92.0 2.5 %copy-start.7 = (bf16[8,4,16,64]{3,0,2,1:T(8,128)(2,1)S(1)}, bf16[8,4,16,64]{3,0,2,1:T(8,128)(2,1)}, u32[]{:S(2)}) copy-start(bf16[8,4,16,64]{3,0,2,1:T(8,128)(2,1)} %constant_dynamic-slice_fusion) | copy-start | bytes 196612

commit v2 on v1

--- a/solution.py
+++ b/solution.py
@@ -217,32 +217,204 @@
     )(x)
 
 
-def convolve(inputs, kernel, specs, padding, lhs_step, rhs_step):
-    return lax.conv_general_dilated(
-        inputs,
-        kernel,
-        (1, 1, 1),
-        padding,
-        lhs_dilation=lhs_step,
-        rhs_dilation=rhs_step,
-        dimension_numbers=specs,
-        preferred_element_type=jnp.float32,
+NT = (((1,), (1,)), ((), ()))
+
+
+def dot(lhs, rhs):
+    return jnp.dot(lhs, rhs, preferred_element_type=jnp.float32)
+
+
+def dot_nt(lhs, rhs):
+    return lax.dot_general(lhs, rhs, NT, preferred_element_type=jnp.float32)
+
+
+def compute_kernel(
+    sizes, mid, rows, cols, diag, k1, kd, terms, grad_clip,
+    wide, even, odd, parts, fine, act, grad, moved, dilated, own,
+):
+    n_t, n_h, n_w = sizes
+    frames = 2 * n_t
+    t, h, w = lax.axis_index("ta"), lax.axis_index("ha"), lax.axis_index("wa")
+    f32, b16 = jnp.float32, jnp.bfloat16
+    ch = mid.shape[-1]
+    share = ch // n_t
+
+    wide[0:2] = jnp.zeros((2, 8, 24, ch), f32)
+    grad[frames : frames + 2] = jnp.zeros((2, 6, 24, ch), f32)
+    act[0:1] = jnp.zeros((1,) + act.shape[1:], f32)
+    dilated[n_t : n_t + 1] = jnp.zeros((1,) + dilated.shape[1:], f32)
+    moved[...] = jnp.zeros(moved.shape, f32)
+
+    out_at = lax.broadcasted_iota(jnp.int32, (72, 24), 0)
+    in_at = lax.broadcasted_iota(jnp.int32, (72, 24), 1)
+    tap = jnp.where(out_at >= 48, 2, jnp.where(out_at >= 24, 1, 0))
+    reach = out_at - 24 * tap - tap
+    hit = (reach == 2 * (in_at - 8))
+    select = jnp.where(hit, 1.0, 0.0).astype(b16)
+    select_own = jnp.where(hit & (in_at >= 8) & (in_at < 16), 1.0, 0.0).astype(b16)
+
+    @pl.loop(0, n_t)
+    def _(s):
+        for f in range(2):
+            for r in range(2):
+                at, k = 2 + 2 * s + f, 2 * f + r
+                wide[at, r, 2:18] = rows[s, 0, 2 + k].astype(f32)
+                wide[at, 2 + r, 2:18] = mid[s, k].astype(f32)
+                wide[at, 4 + r, 2:18] = mid[s, 7 + k].astype(f32)
+                wide[at, 6 + r, 2:18] = rows[s, 1, k].astype(f32)
+        for side in range(2):
+            strips = (diag[s, 0, side, 1], cols[s, side, 0], cols[s, side, 2], diag[s, 1, side, 0])
+            for n, strip in enumerate(strips):
+                strip = strip.astype(f32)
+                for f in range(2):
+                    for r in range(2):
+                        first = 4 * (2 * f + r) + 2 - 2 * side
+                        wide[2 + 2 * s + f, 2 * n + r, 18 * side : 18 * side + 2] = strip[
+                            first : first + 2
+                        ]
+        middle = (
+            (diag[s, 0, 0, 0], rows[s, 0, 0], diag[s, 0, 1, 0]),
+            (cols[s, 0, 1], mid[s, 5], cols[s, 1, 1]),
+            (diag[s, 1, 0, 1], rows[s, 1, 5], diag[s, 1, 1, 1]),
+        )
+        for n, (block, r) in enumerate(((0, 1), (1, 0), (1, 1), (2, 0))):
+            line = jnp.concatenate(
+                [x.astype(f32)[8 * r : 8 * r + 8] for x in middle[block]], axis=0
+            ).astype(b16)
+            spread = dot(select, line)
+            for c in range(3):
+                dilated[s, n, c] = spread[24 * c : 24 * c + 24]
+            if block == 1:
+                spread = dot(select_own, line)
+                for c in range(3):
+                    own[c, s, r] = spread[24 * c : 24 * c + 24]
+
+    @pl.loop(0, frames + 2)
+    def _(f):
+        even[f] = wide[f].reshape(192, ch).astype(b16)
+        odd[f] = wide[f, 1:7].reshape(144, ch).astype(b16)
+
+    def shifted(f, count, b):
+        if b == 1:
+            return odd[pl.ds(f, count)].reshape(count * 144, ch)
+        return even[pl.ds(f, count), 24 * b : 24 * b + 144].reshape(count * 144, ch)
+
+    def weight(ref, a, b, c):
+        return ref[pl.ds(((a * 3 + b) * 3 + c) * ch, ch), :]
+
+    @pl.loop(0, n_t)
+    def _(s):
+        for c in range(3):
+            total = jnp.zeros((288, ch), f32)
+            for a in range(3):
+                for b in range(3):
+                    total += dot(shifted(2 * s + a, 2, b), weight(k1, a, b, c))
+            parts[c, pl.ds(2 * s, 2), :, 0:24] = total.reshape(2, 6, 24, ch)
+
+    for pt in range(2):
+        for ph in range(2):
+            total = jnp.zeros((n_t * 72, ch), f32)
+            for a in (1,) if pt else (0, 2):
+                for b in (1,) if ph else (0, 2):
+                    j = 0 if a == 2 else 1
+                    r = 0 if b == 2 else 1
+                    for c in range(3):
+                        lhs = dilated[j : j + n_t, r : r + 3, c].reshape(n_t * 72, ch)
+                        total += dot_nt(lhs.astype(b16), weight(kd, a, b, c))
+            fine[:, pt, :, ph] = total.reshape(n_t, 3, 24, ch)
+
+    row = lax.broadcasted_iota(jnp.int32, (6, 24, ch), 0) + (h * 4 - 1)
+    place = lax.broadcasted_iota(jnp.int32, (6, 24, ch), 1)
+    col = place + (w * 16 - 1)
+    inside = (row >= 0) & (row < 4 * n_h) & (col >= 0) & (col < 16 * n_w) & (place < 18)
+
+    @pl.loop(0, n_t)
+    def _(s):
+        for k in range(2):
+            f = 2 * s + k
+            pre = parts[0, f, :, 0:24] + parts[1, f, :, 1:25] + parts[2, f, :, 2:26]
+            sigma = 1.0 / (1.0 + jnp.exp(-pre))
+            value = jnp.where(inside, pre * sigma, 0.0)
+            act[s + 1, k] = value.astype(b16).astype(f32).reshape(3, 2, 24, ch)
+            back = fine[s, k].reshape(6, 24, ch) * sigma * (1.0 + pre * (1.0 - sigma))
+            grad[f] = jnp.where(inside, back, 0.0).astype(b16).astype(f32)
+            centre = grad[f, 1:5, 1:17]
+            for c in range(3):
+                moved[c, f, :, 1 + c : 17 + c] = centre
+
+    pick = (
+        lax.broadcasted_iota(jnp.int32, (share, ch), 1)
+        == lax.broadcasted_iota(jnp.int32, (share, ch), 0) + t * share
     )
+    pick = jnp.where(pick, 1.0, 0.0).astype(b16)
+    conv_side = jnp.concatenate(
+        [dot_nt(pick, moved[c].reshape(frames * 96, ch).astype(b16)) for c in range(3)], axis=0
+    ).astype(b16)
+    down_side = jnp.concatenate(
+        [dot_nt(pick, own[c].reshape(n_t * 48, ch).astype(b16)) for c in range(3)], axis=0
+    ).astype(b16)
+    for a in range(3):
+        for b in range(3):
+            if b == 1:
+                lhs = even[a : a + frames, 48:144]
+            else:
+                lhs = odd[a : a + frames, 24 * b : 24 * b + 96]
+            conv = dot(conv_side, lhs.reshape(frames * 96, ch))
+            lhs = act[a // 2 : a // 2 + n_t, a % 2, b // 2 : b // 2 + 2, b % 2]
+            down = dot(down_side, lhs.reshape(n_t * 48, ch).astype(b16))
+            for c in range(3):
+                cut = slice(share * c, share * (c + 1))
+                both = jnp.concatenate([conv[cut], down[cut]], axis=0)
+                at = ((a * 3 + b) * 3 + c) * ch
+                terms[at : at + ch] = both.T.astype(b16)
+
+    sums = [jnp.zeros((192, ch), f32) for _ in range(3)]
+    for c in range(3):
+        for a in range(3):
+            for b in range(3):
+                lhs = grad[pl.ds(2 * t + 2 - a, 2), 2 - b : 6 - b].reshape(192, ch)
+                sums[c] += dot_nt(lhs.astype(b16), weight(k1, a, b, c))
+        parts[c, 0:2, 0:4, 0:24] = sums[c].reshape(2, 4, 24, ch)
+    result = (
+        parts[0, 0:2, 0:4, 2:18] + parts[1, 0:2, 0:4, 1:17] + parts[2, 0:2, 0:4, 0:16]
+    )
+    grad_clip[...] = result.astype(b16)
+
+
+def compute(mid, rows, cols, diag, conv_weight, down_weight, sizes):
+    n_t = sizes[0]
+    frames = 2 * n_t
+    ch = mid.shape[-1]
+    f32, b16 = jnp.float32, jnp.bfloat16
+    vmem = pl.BlockSpec(memory_space=pltpu.VMEM)
+    return pl.pallas_call(
+        functools.partial(compute_kernel, sizes),
+        out_shape=[
+            jax.ShapeDtypeStruct((27 * ch, 2 * ch // n_t), b16),
+            jax.ShapeDtypeStruct((2, 4, 16, ch), b16),
+        ],
+        in_specs=[vmem] * 6,
+        out_specs=[vmem] * 2,
+        scratch_shapes=[
+            pltpu.VMEM((frames + 2, 8, 24, ch), f32),
+            pltpu.VMEM((frames + 2, 192, ch), b16),
+            pltpu.VMEM((frames + 2, 144, ch), b16),
+            pltpu.VMEM((3, frames, 6, 32, ch), f32),
+            pltpu.VMEM((n_t, 2, 3, 2, 24, ch), f32),
+            pltpu.VMEM((n_t + 1, 2, 3, 2, 24, ch), f32),
+            pltpu.VMEM((frames + 2, 6, 24, ch), f32),
+            pltpu.VMEM((3, frames, 4, 24, ch), f32),
+            pltpu.VMEM((n_t + 1, 4, 3, 24, ch), f32),
+            pltpu.VMEM((3, n_t, 2, 24, ch), f32),
+        ],
+        compiler_params=pltpu.CompilerParams(vmem_limit_bytes=56 * 2**20),
+    )(mid, rows, cols, diag, conv_weight, down_weight)
 
 
 def local(clip, conv_weight, down_weight, out_cotangent):
     channels = clip.shape[-1]
     n_t, n_h, n_w = (lax.axis_size(axis) for axis in ("ta", "ha", "wa"))
-    t, h, w = lax.axis_index("ta"), lax.axis_index("ha"), lax.axis_index("wa")
     share = channels // n_t
-    first_kernel = conv_weight.reshape(3, 3, 3, channels, channels)
-    down_kernel = down_weight.reshape(3, 3, 3, channels, channels)
-    unit = (1, 1, 1)
-    valid = [(0, 0), (0, 0), (0, 0)]
-    forward_specs = ("NDHWC", "DHWIO", "NDHWC")
-    back_specs = ("NDHWC", "DHWOI", "NDHWC")
-    weight_specs = ("CDHWN", "IDHWO", "DHWNC")
-
     edges = jnp.concatenate([clip[:, :, :2], clip[:, :, -2:]], axis=2)
     packed = jnp.concatenate(
         [
@@ -255,89 +427,12 @@
         axis=0,
     )
     mid, rows, cols, diag = gather(packed, (n_t, n_h, n_w))
-    frames = 2 * n_t
-
-    def half(chunk):
-        return chunk.reshape(frames, 2, 16, channels)
-
-    def edge(chunk):
-        return chunk.reshape(frames, 2, 4, channels)
-
-    def coarse(chunk):
-        return chunk.reshape(n_t, 2, 8, channels)
-
-    centre = jnp.concatenate(
-        [half(rows[:, 0, 2:6]), half(mid[:, 0:4]), half(mid[:, 7:11]), half(rows[:, 1, 0:4])],
-        axis=1,
+    terms, grad_clip = compute(
+        mid, rows, cols, diag, conv_weight, down_weight, (n_t, n_h, n_w)
     )
-    left, right = (
-        jnp.concatenate(
-            [
-                edge(diag[:, 0, side, 1]),
-                edge(cols[:, side, 0]),
-                edge(cols[:, side, 2]),
-                edge(diag[:, 1, side, 0]),
-            ],
-            axis=1,
-        )
-        for side in (0, 1)
-    )
-    clip_ext = jnp.concatenate([left[:, :, 2:], centre, right[:, :, :2]], axis=2)
-    cot_rows = [
-        jnp.concatenate([coarse(a), coarse(b), coarse(c)], axis=2)
-        for a, b, c in (
-            (diag[:, 0, 0, 0], rows[:, 0, 0], diag[:, 0, 1, 0]),
-            (cols[:, 0, 1], mid[:, 5], cols[:, 1, 1]),
-            (diag[:, 1, 0, 1], rows[:, 1, 5], diag[:, 1, 1, 1]),
-        )
-    ]
-    cot_ext = jnp.concatenate(cot_rows, axis=1)[:, 1:5, 7:17]
-    cot_mid = coarse(mid[:, 5])
-
-    row = lax.broadcasted_iota(jnp.int32, (1, 6, 18, 1), 1) + (h * 4 - 1)
-    col = lax.broadcasted_iota(jnp.int32, (1, 6, 18, 1), 2) + (w * 16 - 1)
-    inside = (row >= 0) & (row < 4 * n_h) & (col >= 0) & (col < 16 * n_w)
-    pre_act = convolve(
-        clip_ext[None], first_kernel, forward_specs, [(2, 0), (0, 0), (0, 0)], unit, unit
-    )[0]
-    grad_act = convolve(
-        cot_ext[None],
-        down_kernel[::-1, ::-1, ::-1],
-        back_specs,
-        [(0, 3), (0, 1), (0, 1)],
-        (2, 2, 2),
-        unit,
-    )[0]
-    sigma = jax.nn.sigmoid(pre_act)
-    activation = jnp.where(inside, pre_act * sigma, 0.0).astype(jnp.bfloat16)
-    grad_pre = jnp.where(
-        inside, grad_act * sigma * (1.0 + pre_act * (1.0 - sigma)), 0.0
-    ).astype(jnp.bfloat16)
-
-    start = t * share
-
-    def blocks(values, depth):
-        ahead = jnp.pad(values, ((2, 0), (0, 0), (0, 0), (0, 0)))
-        return jnp.stack([ahead[2 * i : 2 * i + depth] for i in range(n_t)])
-
-    act_blocks = blocks(activation[:, :5, :17], 3)
-    clip_blocks = blocks(clip_ext[:, 1:7, 1:19], 4)
-    cot_blocks = lax.dynamic_slice_in_dim(cot_mid, start, share, 3)[:, None]
-    grad_mid = lax.dynamic_slice_in_dim(grad_pre[:, 1:5, 1:17], start, share, 3)
-    grad_blocks = grad_mid.reshape(n_t, 2, 4, 16, share)
-    grad_down = convolve(act_blocks, cot_blocks, weight_specs, valid, unit, (2, 2, 2))
-    grad_conv = convolve(clip_blocks, grad_blocks, weight_specs, valid, unit, unit)
-    terms = jnp.concatenate(
-        [grad_conv.reshape(27 * channels, share), grad_down.reshape(27 * channels, share)], axis=1
-    ).astype(jnp.bfloat16)
     terms = terms.reshape(n_h // 2, 2, n_w, 27 * channels // (n_h * n_w), 2 * share)
     total = reduce_scatter(terms, (n_h // 2, n_w))
 
-    later = jnp.pad(grad_pre, ((0, 2), (0, 0), (0, 0), (0, 0)))
-    grad_ext = lax.dynamic_slice_in_dim(later, 2 * t, 4, 0)
-    grad_clip = convolve(
-        grad_ext[None], first_kernel[::-1, ::-1, ::-1], back_specs, valid, unit, unit
-    )[0].astype(jnp.bfloat16)
     return (grad_clip, total[:, :share], total[:, share:])
 
 

time: 127 us -> 58.6 us (0.46); the launches traced: 125 us -> 58.3 us
  local copies, waits for them, and re-layouts: 53.6 us -> 8.58 us
  matrix products: 29.1 us -> 0 us
  Pallas kernels: 32.6 us -> 49 us
  other arithmetic: 8.41 us -> 0.02 us
    another operation x34 -> x0, local copies, waits for them, and re-layouts: 34.5 us -> none  [the longest x16 21.6 us: edge(): return chunk.reshape(frames, 2, 4, channels)]
    conv_general_dilated x5 -> x0, matrix products: 29.1 us -> none  [convolve(): lax.conv_general_dilated(inputs, kernel, (1, 1, 1), padding, lhs_dilation...]
    pallas_call x0 -> x1, Pallas kernels: none -> 16.5 us  [compute(): pl.pallas_call(functools.partial(compute_kernel, sizes), out_shape=[jax.S...]
    concatenate x2 -> x0, other arithmetic: 5.08 us -> none  [the longest x1 2.98 us: local(): jnp.concatenate([grad_conv.reshape(27 * channels, share), grad_down.resha...]
    slice x7 -> x0, local copies, waits for them, and re-layouts: 4.38 us -> none  [the longest x1 1.48 us: local(): cols[:, side, 0]]
    unnamed x31 -> x16, local copies, waits for them, and re-layouts: 8.62 us -> 6.79 us
    broadcast_in_dim x1 -> x0, other arithmetic: 1.53 us -> none  [local(): cot_ext[None]]
    reshape x2 -> x0, local copies, waits for them, and re-layouts: 1.5 us -> none  [half(): return chunk.reshape(frames, 2, 16, channels)]
where the time goes in v2:
time: 58.6 us; the launch traced here: 58.3 us
  Pallas kernels  49 us (84%)
  local copies, waits for them, and re-layouts  8.58 us (15%)
  between operations  0.69 us (1%)
    pallas_call x1, Pallas kernels, gather(): pl.pallas_call(functools.partial(gather_kernel, sizes), out_shape=[jax.Sh...  17.5 us
    pallas_call x1, Pallas kernels, compute(): pl.pallas_call(functools.partial(compute_kernel, sizes), out_shape=[jax.S...  16.5 us
    pallas_call x1, Pallas kernels, reduce_scatter(): pl.pallas_call(functools.partial(reduce_kernel, sizes), out_shape=jax.Sha...  15 us
    unnamed x16, local copies, waits for them, and re-layouts  6.79 us

profile of v2, /device:TPU:0, one launch (start us, length us, event | category | flops | bytes accessed | tf_op | source)
XLA Modules:
  0.0 58.3 jit_solution(8771968834600355864)
XLA Ops:
  0.6 0.8 %fusion.3 = (bf16[2,4,2,256]{3,2,1,0:T(2,128)(2,1)S(1)}, bf16[2,4,2,256]{3,2,1,0:T(2,128)(2,1)S(1)}) fusion(bf16[2,4,16,256]{3,2,1,0:T(8,128)(2,1)} %param.4), kind=kLoop, calls=%fused_computation.11 | loop fusion | bytes 32768 | tf_op jit(solution)/shard_map/slice | solution.py:418
  1.5 0.8 %fusion.2 = (bf16[2,2,16,256]{3,2,1,0:T(8,128)(2,1)S(1)}, bf16[2,2,16,256]{3,2,1,0:T(8,128)(2,1)S(1)}) fusion(bf16[2,4,16,256]{3,2,1,0:T(8,128)(2,1)} %param.4), kind=kLoop, calls=%fused_computation.10 | loop fusion | bytes 131072 | tf_op jit(solution)/shard_map/slice | solution.py:425
  2.3 0.7 %constant_dynamic-update-slice_fusion.2 = bf16[11,16,256]{2,1,0:T(8,128)(2,1)S(1)} fusion(bf16[11,16,256]{2,1,0:T(8,128)(2,1)S(1)} %constant_dynamic-update-slice_fusion.3, bf16[1,2,8,256]{3,2,1,0:T(8,128)(2,1)} %param.7), kind=kLoop, calls=%fused_computation.4 | loop fusion | bytes 16384
  3.0 17.5 %shard_map.67 = (bf16[4,11,16,256]{3,2,1,0:T(8,128)(2,1)S(1)}, bf16[4,2,6,16,256]{4,3,2,1,0:T(8,128)(2,1)S(1)}, bf16[4,2,3,16,256]{4,3,2,1,0:T(8,128)(2,1)S(1)}, bf16[4,2,2,2,16,256]{5,4,3,2,1,0:T(8,128)(2,1)S(1)}) custom-call(bf16[11,16,256]{2,1,0:T(8,128)(2,1)S(1)} %constant_dynamic-update-slice_fusion.x_ref), custom_call_target="tpu_custom_call" | custom-call | tf_op jit(solution)/shard_map/pallas_call | solution.py:118
  20.5 0.0 copy-start.1
  20.5 0.7 %copy-done.1 = bf16[4,2,6,16,256]{4,3,2,1,0:T(8,128)(2,1)} copy-done((bf16[4,2,6,16,256]{4,3,2,1,0:T(8,128)(2,1)}, bf16[4,2,6,16,256]{4,3,2,1,0:T(8,128)(2,1)S(1)}, u32[]{:S(2)}) %copy-start.1) | copy-done | bytes 393240
  21.3 0.0 copy-start.2
  21.3 0.7 %copy-done.2 = bf16[4,11,16,256]{3,2,1,0:T(8,128)(2,1)} copy-done((bf16[4,11,16,256]{3,2,1,0:T(8,128)(2,1)}, bf16[4,11,16,256]{3,2,1,0:T(8,128)(2,1)S(1)}, u32[]{:S(2)}) %copy-start.2) | copy-done | bytes 360472
  22.0 0.0 copy-start.3
  22.0 0.7 %copy-done.3 = bf16[4,2,2,2,16,256]{5,4,3,2,1,0:T(8,128)(2,1)} copy-done((bf16[4,2,2,2,16,256]{5,4,3,2,1,0:T(8,128)(2,1)}, bf16[4,2,2,2,16,256]{5,4,3,2,1,0:T(8,128)(2,1)S(1)}, u32[]{:S(2)}) %copy-start.3) | copy-done | bytes 262168
  22.7 0.0 copy-start.4
  22.7 0.7 %copy-done.4 = bf16[4,2,3,16,256]{4,3,2,1,0:T(8,128)(2,1)} copy-done((bf16[4,2,3,16,256]{4,3,2,1,0:T(8,128)(2,1)}, bf16[4,2,3,16,256]{4,3,2,1,0:T(8,128)(2,1)S(1)}, u32[]{:S(2)}) %copy-start.4) | copy-done | bytes 196632
  23.4 16.5 %shard_map.68 = (bf16[6912,128]{1,0:T(8,128)(2,1)}, bf16[2,4,16,256]{3,2,1,0:T(8,128)(2,1)}) custom-call(bf16[4,11,16,256]{3,2,1,0:T(8,128)(2,1)} %copy-done.2, bf16[4,2,6,16,256]{4,3,2,1,0:T(8,128)(2,1)} %copy-done.1, bf16[4,2,3,16,256]{4,3,2,1,0:T(8,128)(2,1)} %copy-done.4, bf16[4,2,2,2,16,256]{5,4,3,2,1,0:T(8,128)(2,1)} %copy-done.3, ...), custom_call_target="tpu_custom_call" | custom-call | tf_op jit(solution)/shard_map/pallas_call | solution.py:390
  39.9 0.0 copy-start
  39.9 1.5 %copy-done = bf16[6912,128]{1,0:T(8,128)(2,1)S(1)} copy-done((bf16[6912,128]{1,0:T(8,128)(2,1)S(1)}, bf16[6912,128]{1,0:T(8,128)(2,1)}, u32[]{:S(2)}) %copy-start) | copy-done | bytes 1769496
  41.3 15.0 %shard_map.69 = f32[864,128]{1,0:T(8,128)S(1)} custom-call(bf16[2,2,2,864,128]{4,3,2,1,0:T(8,128)(2,1)S(1)} %bitcast.5), custom_call_target="tpu_custom_call" | custom-call | tf_op jit(solution)/shard_map/pallas_call | solution.py:201
  56.3 0.2 fusion.1
  56.5 0.9 %copy.8 = f32[864,64]{0,1:T(8,128)} copy(f32[864,64]{1,0:T(8,128)S(1)} %get-tuple-element.18) | data formatting | bytes 442368
  57.4 0.9 %copy.7 = f32[864,64]{0,1:T(8,128)} copy(f32[864,64]{1,0:T(8,128)S(1)} %get-tuple-element.19) | data formatting | bytes 442368
  (7 shorter events, 0.1 us)
Async XLA Ops:
  20.5 0.8 %copy-start.1 = (bf16[4,2,6,16,256]{4,3,2,1,0:T(8,128)(2,1)}, bf16[4,2,6,16,256]{4,3,2,1,0:T(8,128)(2,1)S(1)}, u32[]{:S(2)}) copy-start(bf16[4,2,6,16,256]{4,3,2,1,0:T(8,128)(2,1)S(1)} %get-tuple-element.10.rows) | copy-start | bytes 1179652
  21.3 0.7 %copy-start.2 = (bf16[4,11,16,256]{3,2,1,0:T(8,128)(2,1)}, bf16[4,11,16,256]{3,2,1,0:T(8,128)(2,1)S(1)}, u32[]{:S(2)}) copy-start(bf16[4,11,16,256]{3,2,1,0:T(8,128)(2,1)S(1)} %get-tuple-element.9.mid) | copy-start | bytes 1081348
  22.0 0.7 %copy-start.3 = (bf16[4,2,2,2,16,256]{5,4,3,2,1,0:T(8,128)(2,1)}, bf16[4,2,2,2,16,256]{5,4,3,2,1,0:T(8,128)(2,1)S(1)}, u32[]{:S(2)}) copy-start(bf16[4,2,2,2,16,256]{5,4,3,2,1,0:T(8,128)(2,1)S(1)} %get-tuple-element.12.diag) | copy-start | bytes 786436
  22.7 0.7 %copy-start.4 = (bf16[4,2,3,16,256]{4,3,2,1,0:T(8,128)(2,1)}, bf16[4,2,3,16,256]{4,3,2,1,0:T(8,128)(2,1)S(1)}, u32[]{:S(2)}) copy-start(bf16[4,2,3,16,256]{4,3,2,1,0:T(8,128)(2,1)S(1)} %get-tuple-element.11.cols) | copy-start | bytes 589828
  39.9 1.5 %copy-start = (bf16[6912,128]{1,0:T(8,128)(2,1)S(1)}, bf16[6912,128]{1,0:T(8,128)(2,1)}, u32[]{:S(2)}) copy-start(bf16[6912,128]{1,0:T(8,128)(2,1)} %get-tuple-element.14) | copy-start | bytes 5308420

commit v3 on v2

v3 whole, which is shorter than its diff:
```python
import functools

import jax
import jax.numpy as jnp
from jax import lax
from jax.experimental import pallas as pl
from jax.experimental.pallas import tpu as pltpu
from jax.sharding import PartitionSpec as P

MESH = pl.DeviceIdType.MESH
SIDES = [(dh, dw) for dh in (-1, 0, 1) for dw in (-1, 0, 1) if (dh, dw) != (0, 0)]
NT = (((1,), (1,)), ((), ()))


def dot(lhs, rhs):
    return jnp.dot(lhs, rhs, preferred_element_type=jnp.float32)


def dot_nt(lhs, rhs):
    return lax.dot_general(lhs, rhs, NT, preferred_element_type=jnp.float32)


def kernel(
    sizes, clip, cot, k1_hbm, kd_hbm, grad_clip, grad_conv, grad_down,
    k1, kd, mid, edge, strip_f32, rows, cols, diag,
    wide, even, odd, parts, fine, act, grad, moved, dilated, own_cot,
    flat, terms, pair, both, got,
    load, zs, zr, ps, pr, pair_sems, ss, rs,
):
    n_t, n_h, n_w = sizes
    frames = 2 * n_t
    t, h, w = lax.axis_index("ta"), lax.axis_index("ha"), lax.axis_index("wa")
    f32, b16 = jnp.float32, jnp.bfloat16
    ch = clip.shape[-1]
    share = ch // n_t
    peers = n_h * n_w
    chips = peers // 2
    core = lax.rem(h, 2)
    me = (h // 2) * n_w + w

    loads = [
        pltpu.make_async_copy(k1_hbm, k1, load.at[0]),
        pltpu.make_async_copy(kd_hbm, kd, load.at[1]),
    ]
    for copy in loads:
        copy.start()

    barrier = pltpu.get_barrier_semaphore()
    for d in range(1, n_t):
        pl.semaphore_signal(
            barrier, inc=1, device_id=(lax.rem(t + d, n_t), h, w), device_id_type=MESH
        )
    for d in range(1, peers):
        peer = lax.rem(h * n_w + w + d, peers)
        pl.semaphore_signal(
            barrier, inc=1, device_id=(t, peer // n_w, lax.rem(peer, n_w)), device_id_type=MESH
        )

    def exists(dh, dw):
        return (h + dh >= 0) & (h + dh < n_h) & (w + dw >= 0) & (w + dw < n_w)

    def slot(s, dh, dw):
        if dw == 0:
            return rows.at[s, 0 if dh > 0 else 1]
        if dh == 0:
            return cols.at[s, 0 if dw > 0 else 1]
        return diag.at[s, 0 if dh > 0 else 1, 0 if dw > 0 else 1]

    def piece(s, dh, dw):
        if dw == 0:
            return mid.at[s, pl.ds(0, 5) if dh < 0 else pl.ds(4, 5)]
        if dh == 0:
            return edge.at[s]
        return edge.at[s, pl.ds(0, 2) if dh < 0 else pl.ds(1, 2)]

    for f in range(2):
        for r in range(2):
            mid[t, 2 * f + r] = clip[f, r]
            mid[t, 5 + 2 * f + r] = clip[f, 2 + r]
    mid[t, 4] = cot[0].reshape(16, ch)

    def pack(s):
        for p in range(2):
            for k in range(4):
                line = mid[s, 5 * p + k].astype(f32)
                strip_f32[p, 4 * k : 4 * k + 2] = line[0:2]
                strip_f32[p, 4 * k + 2 : 4 * k + 4] = line[14:16]
            edge[s, 2 * p] = strip_f32[p].astype(b16)
        edge[s, 1] = mid[s, 4]

    pack(t)
    pl.semaphore_wait(barrier, n_t + peers - 2)

    along = []
    for d in range(1, n_t):
        copy = pltpu.make_async_remote_copy(
            src_ref=mid.at[t],
            dst_ref=mid.at[t],
            send_sem=zs.at[d - 1],
            recv_sem=zr.at[d - 1],
            device_id=(lax.rem(t + d, n_t), h, w),
            device_id_type=MESH,
        )
        copy.start()
        along.append(copy)

    def landing(d):
        s = lax.rem(t - d + n_t, n_t)
        return pltpu.make_async_remote_copy(
            src_ref=mid.at[s],
            dst_ref=mid.at[s],
            send_sem=zs.at[d - 1],
            recv_sem=zr.at[d - 1],
            device_id=(lax.rem(t + d, n_t), h, w),
            device_id_type=MESH,
        )

    def beside(d, i):
        dh, dw = SIDES[i]
        s = lax.rem(t - d + n_t, n_t)
        return pltpu.make_async_remote_copy(
            src_ref=piece(s, dh, dw),
            dst_ref=slot(s, dh, dw),
            send_sem=ps.at[d, i],
            recv_sem=pr.at[d, i],
            device_id=(t, h + dh, w + dw),
            device_id_type=MESH,
        )

    def spread_out(d):
        for i, (dh, dw) in enumerate(SIDES):

            @pl.when(exists(dh, dw))
            def _():
                beside(d, i).start()

    def collect(d):
        for i, (dh, dw) in enumerate(SIDES):

            @pl.when(exists(-dh, -dw))
            def _():
                beside(d, i).wait_recv()

    spread_out(0)
    for i, (dh, dw) in enumerate(SIDES):

        @pl.when(jnp.logical_not(exists(-dh, -dw)))
        def _():
            for block in range(n_t):
                target = slot(block, dh, dw)
                target[...] = jnp.zeros(target.shape, target.dtype)

    wide[0:2] = jnp.zeros((2, 8, 24, ch), f32)
    grad[frames : frames + 2] = jnp.zeros((2, 6, 24, ch), f32)
    act[0:1] = jnp.zeros((1,) + act.shape[1:], f32)
    dilated[n_t : n_t + 1] = jnp.zeros((1,) + dilated.shape[1:], f32)
    moved[...] = jnp.zeros(moved.shape, f32)

    out_at = lax.broadcasted_iota(jnp.int32, (72, 24), 0)
    in_at = lax.broadcasted_iota(jnp.int32, (72, 24), 1)
    tap = jnp.where(out_at >= 48, 2, jnp.where(out_at >= 24, 1, 0))
    reach = out_at - 24 * tap - tap
    hit = (reach == 2 * (in_at - 8))
    select = jnp.where(hit, 1.0, 0.0).astype(b16)
    select_own = jnp.where(hit & (in_at >= 8) & (in_at < 16), 1.0, 0.0).astype(b16)

    def fill(s):
        for f in range(2):
            for r in range(2):
                at, k = 2 + 2 * s + f, 2 * f + r
                wide[at, r, 2:18] = rows[s, 0, 1 + k].astype(f32)
                wide[at, 2 + r, 2:18] = mid[s, k].astype(f32)
                wide[at, 4 + r, 2:18] = mid[s, 5 + k].astype(f32)
                wide[at, 6 + r, 2:18] = rows[s, 1, k].astype(f32)
        for side in range(2):
            strips = (diag[s, 0, side, 1], cols[s, side, 0], cols[s, side, 2], diag[s, 1, side, 0])
            for n, strip in enumerate(strips):
                strip = strip.astype(f32)
                for f in range(2):
                    for r in range(2):
                        first = 4 * (2 * f + r) + 2 - 2 * side
                        wide[2 + 2 * s + f, 2 * n + r, 18 * side : 18 * side + 2] = strip[
                            first : first + 2
                        ]
        middle = (
            (diag[s, 0, 0, 0], rows[s, 0, 0], diag[s, 0, 1, 0]),
            (cols[s, 0, 1], mid[s, 4], cols[s, 1, 1]),
            (diag[s, 1, 0, 1], rows[s, 1, 4], diag[s, 1, 1, 1]),
        )
        for n, (block, r) in enumerate(((0, 1), (1, 0), (1, 1), (2, 0))):
            line = jnp.concatenate(
                [x.astype(f32)[8 * r : 8 * r + 8] for x in middle[block]], axis=0
            ).astype(b16)
            spread = dot(select, line)
            for c in range(3):
                dilated[s, n, c] = spread[24 * c : 24 * c + 24]
            if block == 1:
                spread = dot(select_own, line)
                for c in range(3):
                    own_cot[c, s, r] = spread[24 * c : 24 * c + 24]

    for d in range(1, n_t + 1):
        if d < n_t:
            landing(d).wait_recv()
            pack(lax.rem(t - d + n_t, n_t))
            spread_out(d)
        collect(d - 1)
        fill(lax.rem(t - d + 1 + n_t, n_t))

    @pl.loop(0, frames + 2)
    def _(f):
        even[f] = wide[f].reshape(192, ch).astype(b16)
        odd[f] = wide[f, 1:7].reshape(144, ch).astype(b16)

    def shifted(f, count, b):
        if b == 1:
            return odd[pl.ds(f, count)].reshape(count * 144, ch)
        return even[pl.ds(f, count), 24 * b : 24 * b + 144].reshape(count * 144, ch)

    def weight(ref, a, b, c):
        return ref[pl.ds(((a * 3 + b) * 3 + c) * ch, ch), :]

    loads[0].wait()

    @pl.loop(0, n_t)
    def _(s):
        for c in range(3):
            total = jnp.zeros((288, ch), f32)
            for a in range(3):
                for b in range(3):
                    total += dot(shifted(2 * s + a, 2, b), weight(k1, a, b, c))
            parts[c, pl.ds(2 * s, 2), :, 0:24] = total.reshape(2, 6, 24, ch)

    row = lax.broadcasted_iota(jnp.int32, (6, 24, ch), 0) + (h * 4 - 1)
    place = lax.broadcasted_iota(jnp.int32, (6, 24, ch), 1)
    col = place + (w * 16 - 1)
    inside = (row >= 0) & (row < 4 * n_h) & (col >= 0) & (col < 16 * n_w) & (place < 18)

    @pl.loop(0, n_t)
    def _(s):
        for k in range(2):
            f = 2 * s + k
            pre = parts[0, f, :, 0:24] + parts[1, f, :, 1:25] + parts[2, f, :, 2:26]
            parts[0, f, :, 0:24] = pre
            sigma = 1.0 / (1.0 + jnp.exp(-pre))
            value = jnp.where(inside, pre * sigma, 0.0)
            act[s + 1, k] = value.astype(b16).astype(f32).reshape(3, 2, 24, ch)

    pick = (
        lax.broadcasted_iota(jnp.int32, (share, ch), 1)
        == lax.broadcasted_iota(jnp.int32, (share, ch), 0) + t * share
    )
    pick = jnp.where(pick, 1.0, 0.0).astype(b16)
    width = 27 * ch // peers
    down_side = jnp.concatenate(
        [dot_nt(pick, own_cot[c].reshape(n_t * 48, ch).astype(b16)) for c in range(3)], axis=0
    ).astype(b16)
    for a in range(3):
        for b in range(3):
            lhs = act[a // 2 : a // 2 + n_t, a % 2, b // 2 : b // 2 + 2, b % 2]
            down = dot(down_side, lhs.reshape(n_t * 48, ch).astype(b16))
            for c in range(3):
                at = ((a * 3 + b) * 3 + c) * ch
                flat[0, :, at : at + ch] = down[share * c : share * (c + 1)]

    def place(d):
        chip = lax.rem(me + d, chips)
        return (t, (chip // n_w) * 2 + core, lax.rem(chip, n_w))

    other = (t, h + 1 - 2 * core, w)

    def target(d, on):
        chip = lax.rem(me + d, chips)
        return (chip // n_w) * 2 * n_w + on * n_w + lax.rem(chip, n_w)

    def swap(n, d):
        return pltpu.make_async_remote_copy(
            src_ref=terms.at[n, target(d, 1 - core)],
            dst_ref=pair.at[n, lax.rem(me + d, chips)],
            send_sem=pair_sems.at[0, n, d],
            recv_sem=pair_sems.at[1, n, d],
            device_id=other,
            device_id_type=MESH,
        )

    def send(n, d):
        return pltpu.make_async_remote_copy(
            src_ref=both.at[n, d],
            dst_ref=got.at[n, d],
            send_sem=ss.at[n, d],
            recv_sem=rs.at[n, d],
            device_id=place(d),
            device_id_type=MESH,
        )

    order = list(range(1, chips)) + [0]
    outs = (grad_down, grad_conv)

    def swap_all(n):
        for k in range(peers):
            terms[n, k] = flat[n, :, width * k : width * (k + 1)].astype(b16)
        for d in order:
            swap(n, d).start()

    def send_all(n):
        for d in order:
            swap(n, d).wait_recv()
            mine = terms[n, target(d, core)].astype(f32)
            summed = mine + pair[n, lax.rem(me + d, chips)].astype(f32)
            if d > 0:
                both[n, d] = summed.astype(b16)
                send(n, d).start()
            else:
                outs[n][...] = summed

    def finish(n):
        for d in range(1, chips):
            send(n, d).wait_recv()
            outs[n][...] += got[n, d].astype(f32)

    swap_all(0)
    loads[1].wait()

    for pt in range(2):
        for ph in range(2):
            total = jnp.zeros((n_t * 72, ch), f32)
            for a in (1,) if pt else (0, 2):
                for b in (1,) if ph else (0, 2):
                    j = 0 if a == 2 else 1
                    r = 0 if b == 2 else 1
                    for c in range(3):
                        lhs = dilated[j : j + n_t, r : r + 3, c].reshape(n_t * 72, ch)
                        total += dot_nt(lhs.astype(b16), weight(kd, a, b, c))
            fine[:, pt, :, ph] = total.reshape(n_t, 3, 24, ch)

    send_all(0)

    @pl.loop(0, n_t)
    def _(s):
        for k in range(2):
            f = 2 * s + k
            pre = parts[0, f, :, 0:24]
            sigma = 1.0 / (1.0 + jnp.exp(-pre))
            back = fine[s, k].reshape(6, 24, ch) * sigma * (1.0 + pre * (1.0 - sigma))
            grad[f] = jnp.where(inside, back, 0.0).astype(b16).astype(f32)
            centre = grad[f, 1:5, 1:17]
            for c in range(3):
                moved[c, f, :, 1 + c : 17 + c] = centre

    conv_side = jnp.concatenate(
        [dot_nt(pick, moved[c].reshape(frames * 96, ch).astype(b16)) for c in range(3)], axis=0
    ).astype(b16)
    for a in range(3):
        for b in range(3):
            if b == 1:
                lhs = even[a : a + frames, 48:144]
            else:
                lhs = odd[a : a + frames, 24 * b : 24 * b + 96]
            conv = dot(conv_side, lhs.reshape(frames * 96, ch))
            for c in range(3):
                at = ((a * 3 + b) * 3 + c) * ch
                flat[1, :, at : at + ch] = conv[share * c : share * (c + 1)]

    swap_all(1)

    def clip_part(c):
        total = jnp.zeros((192, ch), f32)
        for a in range(3):
            for b in range(3):
                lhs = grad[pl.ds(2 * t + 2 - a, 2), 2 - b : 6 - b].reshape(192, ch)
                total += dot_nt(lhs.astype(b16), weight(k1, a, b, c))
        parts[c, 0:2, 0:4, 0:24] = total.reshape(2, 4, 24, ch)

    clip_part(0)
    send_all(1)
    clip_part(1)
    clip_part(2)
    result = (
        parts[0, 0:2, 0:4, 2:18] + parts[1, 0:2, 0:4, 1:17] + parts[2, 0:2, 0:4, 0:16]
    )
    grad_clip[...] = result.astype(b16)
    finish(0)
    finish(1)

    for d in range(n_t):
        if d > 0:
            along[d - 1].wait_send()
        for i, (dh, dw) in enumerate(SIDES):

            @pl.when(exists(dh, dw))
            def _():
                beside(d, i).wait_send()

    for n in range(2):
        for d in range(chips):
            swap(n, d).wait_send()
            if d > 0:
                send(n, d).wait_send()


def local(clip, conv_weight, down_weight, out_cotangent):
    ch = clip.shape[-1]
    n_t, n_h, n_w = (lax.axis_size(axis) for axis in ("ta", "ha", "wa"))
    frames = 2 * n_t
    share = ch // n_t
    peers = n_h * n_w
    chips = peers // 2
    width = 27 * ch // peers
    f32, b16 = jnp.float32, jnp.bfloat16
    vmem = pl.BlockSpec(memory_space=pltpu.VMEM)
    hbm = pl.BlockSpec(memory_space=pl.ANY)
    dma = pltpu.SemaphoreType.DMA
    grad_clip, grad_conv, grad_down = pl.pallas_call(
        functools.partial(kernel, (n_t, n_h, n_w)),
        out_shape=[
            jax.ShapeDtypeStruct(clip.shape, b16),
            jax.ShapeDtypeStruct((share, width), f32),
            jax.ShapeDtypeStruct((share, width), f32),
        ],
        in_specs=[vmem, vmem, hbm, hbm],
        out_specs=[vmem] * 3,
        scratch_shapes=[
            pltpu.VMEM((27 * ch, ch), b16),
            pltpu.VMEM((27 * ch, ch), b16),
            pltpu.VMEM((n_t, 9, 16, ch), b16),
            pltpu.VMEM((n_t, 3, 16, ch), b16),
            pltpu.VMEM((2, 16, ch), f32),
            pltpu.VMEM((n_t, 2, 5, 16, ch), b16),
            pltpu.VMEM((n_t, 2, 3, 16, ch), b16),
            pltpu.VMEM((n_t, 2, 2, 2, 16, ch), b16),
            pltpu.VMEM((frames + 2, 8, 24, ch), f32),
            pltpu.VMEM((frames + 2, 192, ch), b16),
            pltpu.VMEM((frames + 2, 144, ch), b16),
            pltpu.VMEM((3, frames, 6, 32, ch), f32),
            pltpu.VMEM((n_t, 2, 3, 2, 24, ch), f32),
            pltpu.VMEM((n_t + 1, 2, 3, 2, 24, ch), f32),
            pltpu.VMEM((frames + 2, 6, 24, ch), f32),
            pltpu.VMEM((3, frames, 4, 24, ch), f32),
            pltpu.VMEM((n_t + 1, 4, 3, 24, ch), f32),
            pltpu.VMEM((3, n_t, 2, 24, ch), f32),
            pltpu.VMEM((2, share, 27 * ch), f32),
            pltpu.VMEM((2, peers, share, width), b16),
            pltpu.VMEM((2, chips, share, width), b16),
            pltpu.VMEM((2, chips, share, width), b16),
            pltpu.VMEM((2, chips, share, width), b16),
            dma((2,)),
            dma((n_t - 1,)),
            dma((n_t - 1,)),
            dma((n_t, 8)),
            dma((n_t, 8)),
            dma((2, 2, chips)),
            dma((2, chips)),
            dma((2, chips)),
        ],
        compiler_params=pltpu.CompilerParams(
            collective_id=0, has_side_effects=True, vmem_limit_bytes=56 * 2**20
        ),
    )(clip, out_cotangent, conv_weight, down_weight)
    return (grad_clip, grad_conv.T, grad_down.T)


def solution(mesh):
    return jax.shard_map(
        local,
        mesh=mesh,
        in_specs=(P("ta", "ha", "wa", None), P(), P(), P("ta", "ha", "wa", None)),
        out_specs=(P("ta", "ha", "wa", None), P(("ha", "wa"), "ta"), P(("ha", "wa"), "ta")),
        check_vma=False,
    )
```

time: 58.6 us -> 45 us (0.77)
  Pallas kernels: 49 us -> 39.3 us
  local copies, waits for them, and re-layouts: 8.58 us -> 4.75 us
    pallas_call x3 -> x1, Pallas kernels: 49 us -> 39.3 us  [local(): pl.pallas_call(functools.partial(kernel, (n_t, n_h, n_w)), out_shape=[jax...]
    unnamed x16 -> x3, local copies, waits for them, and re-layouts: 6.79 us -> 4.75 us
    slice x3 -> x0, local copies, waits for them, and re-layouts: 1.77 us -> none  [the longest x1 0.8 us: local(): edges = jnp.concatenate([clip[:, :, :2], clip[:, :, -2:]], axis=2)]
where the time goes in v3:
time: 45 us; the launch traced here: 44.7 us
  Pallas kernels  39.3 us (87%)
  local copies, waits for them, and re-layouts  4.75 us (11%)
  between operations  0.64 us (1%)
    pallas_call x1, Pallas kernels, local(): pl.pallas_call(functools.partial(kernel, (n_t, n_h, n_w)), out_shape=[jax...  39.3 us
    unnamed x3, local copies, waits for them, and re-layouts  4.75 us

profile of v3, /device:TPU:0, one launch (start us, length us, event | category | flops | bytes accessed | tf_op | source)
XLA Modules:
  0.0 44.7 jit_solution(16866947837207855950)
XLA Ops:
  0.6 39.3 %shard_map.67 = (bf16[2,4,16,256]{3,2,1,0:T(8,128)(2,1)}, f32[64,864]{1,0:T(8,128)}, f32[64,864]{1,0:T(8,128)}) custom-call(bf16[2,4,16,256]{3,2,1,0:T(8,128)(2,1)} %clip.1, bf16[1,2,8,256]{3,2,1,0:T(8,128)(2,1)} %cot.1, bf16[6912,256]{1,0:T(8,128)(2,1)} %k1_hbm.1, bf16[6912,256]{1,0:T(8,128)(2,1)} %kd_hbm.1), custom_call_target="tpu_custom_call" | custom-call | tf_op jit(solution)/shard_map/pallas_call | solution.py:413
  40.0 1.5 %copy.10 = bf16[2,4,16,256]{3,2,1,0:T(8,128)(2,1)} copy(bf16[2,4,16,256]{3,2,1,0:T(8,128)(2,1)} %get-tuple-element.12) | data formatting | bytes 131072
  41.4 1.6 %copy.11 = f32[864,64]{0,1:T(8,128)} copy(f32[864,64]{0,1:T(8,128)} %bitcast.3) | data formatting | bytes 442368
  43.1 1.6 %copy.12 = f32[864,64]{0,1:T(8,128)} copy(f32[864,64]{0,1:T(8,128)} %bitcast.2) | data formatting | bytes 442368

commit v4 on v3

--- a/solution.py
+++ b/solution.py
@@ -199,37 +199,46 @@
                 for c in range(3):
                     own_cot[c, s, r] = spread[24 * c : 24 * c + 24]
 
+    def stack(f):
+        even[f] = wide[f].reshape(192, ch).astype(b16)
+        odd[f] = wide[f, 1:7].reshape(144, ch).astype(b16)
+
+    def shifted(f, count, b):
+        if b == 1:
+            return odd[pl.ds(f, count)].reshape(count * 144, ch)
+        return even[pl.ds(f, count), 24 * b : 24 * b + 144].reshape(count * 144, ch)
+
+    def weight(ref, a, b, c):
+        return ref[pl.ds(((a * 3 + b) * 3 + c) * ch, ch), :]
+
+    def block_pre(s):
+        for c in range(3):
+            total = jnp.zeros((288, ch), f32)
+            for a in range(3):
+                for b in range(3):
+                    total += dot(shifted(2 * s + a, 2, b), weight(k1, a, b, c))
+            parts[c, pl.ds(2 * s, 2), :, 0:24] = total.reshape(2, 6, 24, ch)
+
+    stack(0)
+    stack(1)
     for d in range(1, n_t + 1):
         if d < n_t:
             landing(d).wait_recv()
             pack(lax.rem(t - d + n_t, n_t))
             spread_out(d)
         collect(d - 1)
-        fill(lax.rem(t - d + 1 + n_t, n_t))
-
-    @pl.loop(0, frames + 2)
-    def _(f):
-        even[f] = wide[f].reshape(192, ch).astype(b16)
-        odd[f] = wide[f, 1:7].reshape(144, ch).astype(b16)
-
-    def shifted(f, count, b):
-        if b == 1:
-            return odd[pl.ds(f, count)].reshape(count * 144, ch)
-        return even[pl.ds(f, count), 24 * b : 24 * b + 144].reshape(count * 144, ch)
-
-    def weight(ref, a, b, c):
-        return ref[pl.ds(((a * 3 + b) * 3 + c) * ch, ch), :]
-
-    loads[0].wait()
-
-    @pl.loop(0, n_t)
-    def _(s):
-        for c in range(3):
-            total = jnp.zeros((288, ch), f32)
-            for a in range(3):
-                for b in range(3):
-                    total += dot(shifted(2 * s + a, 2, b), weight(k1, a, b, c))
-            parts[c, pl.ds(2 * s, 2), :, 0:24] = total.reshape(2, 6, 24, ch)
+        block = lax.rem(t - d + 1 + n_t, n_t)
+        fill(block)
+        stack(2 + 2 * block)
+        stack(3 + 2 * block)
+        if d == 1:
+            loads[0].wait()
+        elif d < n_t:
+            block_pre(lax.rem(t - d + 2 + n_t, n_t))
+
+    @pl.loop(0, 2)
+    def _(n):
+        block_pre(lax.rem(t + 1 + n, n_t))
 
     row = lax.broadcasted_iota(jnp.int32, (6, 24, ch), 0) + (h * 4 - 1)
     place = lax.broadcasted_iota(jnp.int32, (6, 24, ch), 1)
@@ -255,30 +264,21 @@
     down_side = jnp.concatenate(
         [dot_nt(pick, own_cot[c].reshape(n_t * 48, ch).astype(b16)) for c in range(3)], axis=0
     ).astype(b16)
-    for a in range(3):
-        for b in range(3):
-            lhs = act[a // 2 : a // 2 + n_t, a % 2, b // 2 : b // 2 + 2, b % 2]
-            down = dot(down_side, lhs.reshape(n_t * 48, ch).astype(b16))
-            for c in range(3):
-                at = ((a * 3 + b) * 3 + c) * ch
-                flat[0, :, at : at + ch] = down[share * c : share * (c + 1)]
-
     def place(d):
         chip = lax.rem(me + d, chips)
         return (t, (chip // n_w) * 2 + core, lax.rem(chip, n_w))
 
     other = (t, h + 1 - 2 * core, w)
 
-    def target(d, on):
-        chip = lax.rem(me + d, chips)
-        return (chip // n_w) * 2 * n_w + on * n_w + lax.rem(chip, n_w)
-
-    def swap(n, d):
+    def target(chip, on):
+        return (chip // n_w) * 2 * n_w + on * n_w + chip % n_w
+
+    def swap(n, chip):
         return pltpu.make_async_remote_copy(
-            src_ref=terms.at[n, target(d, 1 - core)],
-            dst_ref=pair.at[n, lax.rem(me + d, chips)],
-            send_sem=pair_sems.at[0, n, d],
-            recv_sem=pair_sems.at[1, n, d],
+            src_ref=terms.at[n, target(chip, 1 - core)],
+            dst_ref=pair.at[n, chip],
+            send_sem=pair_sems.at[0, n, chip],
+            recv_sem=pair_sems.at[1, n, chip],
             device_id=other,
             device_id_type=MESH,
         )
@@ -296,17 +296,20 @@
     order = list(range(1, chips)) + [0]
     outs = (grad_down, grad_conv)
 
-    def swap_all(n):
-        for k in range(peers):
-            terms[n, k] = flat[n, :, width * k : width * (k + 1)].astype(b16)
-        for d in order:
-            swap(n, d).start()
+    def swap_ready(n, before, done):
+        for chip in range(chips):
+            last = target(chip, 1)
+            if before < width * (last + 1) <= done:
+                for k in (target(chip, 0), last):
+                    terms[n, k] = flat[n, :, width * k : width * (k + 1)].astype(b16)
+                swap(n, chip).start()
 
     def send_all(n):
         for d in order:
-            swap(n, d).wait_recv()
-            mine = terms[n, target(d, core)].astype(f32)
-            summed = mine + pair[n, lax.rem(me + d, chips)].astype(f32)
+            chip = lax.rem(me + d, chips)
+            swap(n, chip).wait_recv()
+            mine = terms[n, target(chip, core)].astype(f32)
+            summed = mine + pair[n, chip].astype(f32)
             if d > 0:
                 both[n, d] = summed.astype(b16)
                 send(n, d).start()
@@ -318,7 +321,15 @@
             send(n, d).wait_recv()
             outs[n][...] += got[n, d].astype(f32)
 
-    swap_all(0)
+    for a in range(3):
+        for b in range(3):
+            lhs = act[a // 2 : a // 2 + n_t, a % 2, b // 2 : b // 2 + 2, b % 2]
+            down = dot(down_side, lhs.reshape(n_t * 48, ch).astype(b16))
+            for c in range(3):
+                at = ((a * 3 + b) * 3 + c) * ch
+                flat[0, :, at : at + ch] = down[share * c : share * (c + 1)]
+            swap_ready(0, (a * 3 + b) * 3 * ch, (a * 3 + b + 1) * 3 * ch)
+
     loads[1].wait()
 
     for pt in range(2):
@@ -360,8 +371,7 @@
             for c in range(3):
                 at = ((a * 3 + b) * 3 + c) * ch
                 flat[1, :, at : at + ch] = conv[share * c : share * (c + 1)]
-
-    swap_all(1)
+            swap_ready(1, (a * 3 + b) * 3 * ch, (a * 3 + b + 1) * 3 * ch)
 
     def clip_part(c):
         total = jnp.zeros((192, ch), f32)
@@ -396,6 +406,17 @@
             swap(n, d).wait_send()
             if d > 0:
                 send(n, d).wait_send()
+
+
+def hand_over(a_in, b_in, c_in, a_out, b_out, c_out, sems):
+    copies = [
+        pltpu.make_async_copy(source, place, sems.at[n])
+        for n, (source, place) in enumerate(((a_in, a_out), (b_in, b_out), (c_in, c_out)))
+    ]
+    for copy in copies:
+        copy.start()
+    for copy in copies:
+        copy.wait()
 
 
 def local(clip, conv_weight, down_weight, out_cotangent):
@@ -453,9 +474,16 @@
             dma((2, chips)),
         ],
         compiler_params=pltpu.CompilerParams(
-            collective_id=0, has_side_effects=True, vmem_limit_bytes=56 * 2**20
+            collective_id=0, has_side_effects=True, vmem_limit_bytes=53 * 2**20
         ),
     )(clip, out_cotangent, conv_weight, down_weight)
+    grad_clip, grad_conv, grad_down = pl.pallas_call(
+        hand_over,
+        out_shape=[jax.ShapeDtypeStruct(x.shape, x.dtype) for x in (grad_clip, grad_conv, grad_down)],
+        in_specs=[hbm] * 3,
+        out_specs=[hbm] * 3,
+        scratch_shapes=[dma((3,))],
+    )(grad_clip, grad_conv, grad_down)
     return (grad_clip, grad_conv.T, grad_down.T)
 
 

time: 45 us -> 58 us (1.29)
  Pallas kernels: 39.3 us -> 53.6 us
  local copies, waits for them, and re-layouts: 4.75 us -> 3.51 us
    pallas_call x0 -> x1, Pallas kernels: none -> 17 us  [local(): pl.pallas_call(hand_over, out_shape=[jax.ShapeDtypeStruct(x.shape, x.dtyp...]
    pallas_call x1, Pallas kernels: 39.3 us -> 36.6 us  [local(): pl.pallas_call(functools.partial(kernel, (n_t, n_h, n_w)), out_shape=[jax...]
    unnamed x3 -> x10, local copies, waits for them, and re-layouts: 4.75 us -> 3.51 us
where the time goes in v4:
time: 58 us; the launch traced here: 57.8 us
  Pallas kernels  53.6 us (92%)
  local copies, waits for them, and re-layouts  3.51 us (6%)
  between operations  0.66 us (1%)
    pallas_call x1, Pallas kernels, local(): pl.pallas_call(functools.partial(kernel, (n_t, n_h, n_w)), out_shape=[jax...  36.6 us
    pallas_call x1, Pallas kernels, local(): pl.pallas_call(hand_over, out_shape=[jax.ShapeDtypeStruct(x.shape, x.dtyp...  17 us
    unnamed x10, local copies, waits for them, and re-layouts  3.51 us

profile of v4, /device:TPU:0, one launch (start us, length us, event | category | flops | bytes accessed | tf_op | source)
XLA Modules:
  0.0 57.8 jit_solution(329137303197252233)
XLA Ops:
  0.6 0.0 copy-start.2
  0.6 0.8 %copy-done.2 = bf16[2,4,16,256]{3,2,1,0:T(8,128)(2,1)S(1)} copy-done((bf16[2,4,16,256]{3,2,1,0:T(8,128)(2,1)S(1)}, bf16[2,4,16,256]{3,2,1,0:T(8,128)(2,1)}, u32[]{:S(2)}) %copy-start.2) | copy-done | bytes 65560
  1.5 0.0 copy-start.4
  1.5 0.7 %copy-done.4 = bf16[1,2,8,256]{3,2,1,0:T(8,128)(2,1)S(1)} copy-done((bf16[1,2,8,256]{3,2,1,0:T(8,128)(2,1)S(1)}, bf16[1,2,8,256]{3,2,1,0:T(8,128)(2,1)}, u32[]{:S(2)}) %copy-start.4) | copy-done | bytes 8216
  2.2 36.6 %shard_map.67 = (bf16[2,4,16,256]{3,2,1,0:T(8,128)(2,1)S(1)}, f32[64,864]{1,0:T(8,128)S(1)}, f32[64,864]{1,0:T(8,128)S(1)}) custom-call(bf16[2,4,16,256]{3,2,1,0:T(8,128)(2,1)S(1)} %copy-done.2, bf16[1,2,8,256]{3,2,1,0:T(8,128)(2,1)S(1)} %copy-done.4, bf16[6912,256]{1,0:T(8,128)(2,1)} %k1_hbm.1, bf16[6912,256]{1,0:T(8,128)(2,1)} %kd_hbm.1), custom_call_target="tpu_custom_call" | custom-call | tf_op jit(solution)/shard_map/pallas_call | solution.py:434
  38.8 0.0 copy-start
  38.8 0.7 %copy-done = f32[64,864]{1,0:T(8,128)} copy-done((f32[64,864]{1,0:T(8,128)}, f32[64,864]{1,0:T(8,128)S(1)}, u32[]{:S(2)}) %copy-start) | copy-done | bytes 221208
  39.5 0.0 copy-start.1
  39.5 0.7 %copy-done.1 = f32[64,864]{1,0:T(8,128)} copy-done((f32[64,864]{1,0:T(8,128)}, f32[64,864]{1,0:T(8,128)S(1)}, u32[]{:S(2)}) %copy-start.1) | copy-done | bytes 221208
  40.1 0.0 copy-start.3
  40.1 0.6 %copy-done.3 = bf16[2,4,16,256]{3,2,1,0:T(8,128)(2,1)} copy-done((bf16[2,4,16,256]{3,2,1,0:T(8,128)(2,1)}, bf16[2,4,16,256]{3,2,1,0:T(8,128)(2,1)S(1)}, u32[]{:S(2)}) %copy-start.3) | copy-done | bytes 65560
  40.8 17.0 %shard_map.68 = (bf16[2,4,16,256]{3,2,1,0:T(8,128)(2,1)}, f32[64,864]{1,0:T(8,128)}, f32[64,864]{1,0:T(8,128)}) custom-call(bf16[2,4,16,256]{3,2,1,0:T(8,128)(2,1)} %copy-done.3, f32[64,864]{1,0:T(8,128)} %copy-done, f32[64,864]{1,0:T(8,128)} %copy-done.1), custom_call_target="tpu_custom_call" | custom-call | tf_op jit(solution)/shard_map/pallas_call | solution.py:480
Async XLA Ops:
  0.6 0.8 %copy-start.2 = (bf16[2,4,16,256]{3,2,1,0:T(8,128)(2,1)S(1)}, bf16[2,4,16,256]{3,2,1,0:T(8,128)(2,1)}, u32[]{:S(2)}) copy-start(bf16[2,4,16,256]{3,2,1,0:T(8,128)(2,1)} %clip.1) | copy-start | bytes 196612
  1.5 0.7 %copy-start.4 = (bf16[1,2,8,256]{3,2,1,0:T(8,128)(2,1)S(1)}, bf16[1,2,8,256]{3,2,1,0:T(8,128)(2,1)}, u32[]{:S(2)}) copy-start(bf16[1,2,8,256]{3,2,1,0:T(8,128)(2,1)} %cot.1) | copy-start | bytes 24580
  38.8 0.7 %copy-start = (f32[64,864]{1,0:T(8,128)}, f32[64,864]{1,0:T(8,128)S(1)}, u32[]{:S(2)}) copy-start(f32[64,864]{1,0:T(8,128)S(1)} %get-tuple-element.10.b_in) | copy-start | bytes 663556
  39.5 0.7 %copy-start.1 = (f32[64,864]{1,0:T(8,128)}, f32[64,864]{1,0:T(8,128)S(1)}, u32[]{:S(2)}) copy-start(f32[64,864]{1,0:T(8,128)S(1)} %get-tuple-element.11.c_in) | copy-start | bytes 663556
  40.1 0.6 %copy-start.3 = (bf16[2,4,16,256]{3,2,1,0:T(8,128)(2,1)}, bf16[2,4,16,256]{3,2,1,0:T(8,128)(2,1)S(1)}, u32[]{:S(2)}) copy-start(bf16[2,4,16,256]{3,2,1,0:T(8,128)(2,1)S(1)} %get-tuple-element.9.a_in) | copy-start | bytes 196612

commit v5 on v4

--- a/solution.py
+++ b/solution.py
@@ -343,8 +343,8 @@
                         lhs = dilated[j : j + n_t, r : r + 3, c].reshape(n_t * 72, ch)
                         total += dot_nt(lhs.astype(b16), weight(kd, a, b, c))
             fine[:, pt, :, ph] = total.reshape(n_t, 3, 24, ch)
-
-    send_all(0)
+        if pt == 0:
+            send_all(0)
 
     @pl.loop(0, n_t)
     def _(s):
@@ -408,15 +408,10 @@
                 send(n, d).wait_send()
 
 
-def hand_over(a_in, b_in, c_in, a_out, b_out, c_out, sems):
-    copies = [
-        pltpu.make_async_copy(source, place, sems.at[n])
-        for n, (source, place) in enumerate(((a_in, a_out), (b_in, b_out), (c_in, c_out)))
-    ]
-    for copy in copies:
-        copy.start()
-    for copy in copies:
-        copy.wait()
+def hand_over(a_in, b_in, c_in, a_out, b_out, c_out):
+    a_out[...] = a_in[...]
+    b_out[...] = b_in[...]
+    c_out[...] = c_in[...]
 
 
 def local(clip, conv_weight, down_weight, out_cotangent):
@@ -480,9 +475,9 @@
     grad_clip, grad_conv, grad_down = pl.pallas_call(
         hand_over,
         out_shape=[jax.ShapeDtypeStruct(x.shape, x.dtype) for x in (grad_clip, grad_conv, grad_down)],
-        in_specs=[hbm] * 3,
-        out_specs=[hbm] * 3,
-        scratch_shapes=[dma((3,))],
+        in_specs=[vmem] * 3,
+        out_specs=[vmem] * 3,
+        compiler_params=pltpu.CompilerParams(vmem_limit_bytes=4 * 2**20),
     )(grad_clip, grad_conv, grad_down)
     return (grad_clip, grad_conv.T, grad_down.T)
 

time: 58 us -> 39.6 us (0.68)
  Pallas kernels: 53.6 us -> 37.2 us
  local copies, waits for them, and re-layouts: 3.51 us -> 1.53 us
    pallas_call x1, Pallas kernels: 17 us -> 0.82 us  [local(): pl.pallas_call(hand_over, out_shape=[jax.ShapeDtypeStruct(x.shape, x.dtyp...]
    unnamed x10 -> x4, local copies, waits for them, and re-layouts: 3.51 us -> 1.53 us
where the time goes in v5:
time: 39.6 us; the launch traced here: 39.4 us
  Pallas kernels  37.2 us (94%)
  local copies, waits for them, and re-layouts  1.53 us (4%)
  between operations  0.65 us (2%)
    pallas_call x1, Pallas kernels, local(): pl.pallas_call(functools.partial(kernel, (n_t, n_h, n_w)), out_shape=[jax...  36.4 us
    unnamed x4, local copies, waits for them, and re-layouts  1.53 us
    pallas_call x1, Pallas kernels, local(): pl.pallas_call(hand_over, out_shape=[jax.ShapeDtypeStruct(x.shape, x.dtyp...  0.82 us

profile of v5, /device:TPU:0, one launch (start us, length us, event | category | flops | bytes accessed | tf_op | source)
XLA Modules:
  0.0 39.4 jit_solution(10853529075764777934)
XLA Ops:
  0.6 0.0 copy-start
  0.6 0.8 %copy-done = bf16[2,4,16,256]{3,2,1,0:T(8,128)(2,1)S(1)} copy-done((bf16[2,4,16,256]{3,2,1,0:T(8,128)(2,1)S(1)}, bf16[2,4,16,256]{3,2,1,0:T(8,128)(2,1)}, u32[]{:S(2)}) %copy-start) | copy-done | bytes 65560
  1.5 0.0 copy-start.1
  1.5 0.7 %copy-done.1 = bf16[1,2,8,256]{3,2,1,0:T(8,128)(2,1)S(1)} copy-done((bf16[1,2,8,256]{3,2,1,0:T(8,128)(2,1)S(1)}, bf16[1,2,8,256]{3,2,1,0:T(8,128)(2,1)}, u32[]{:S(2)}) %copy-start.1) | copy-done | bytes 8216
  2.2 36.4 %shard_map.67 = (bf16[2,4,16,256]{3,2,1,0:T(8,128)(2,1)S(1)}, f32[64,864]{1,0:T(8,128)S(1)}, f32[64,864]{1,0:T(8,128)S(1)}) custom-call(bf16[2,4,16,256]{3,2,1,0:T(8,128)(2,1)S(1)} %copy-done, bf16[1,2,8,256]{3,2,1,0:T(8,128)(2,1)S(1)} %copy-done.1, bf16[6912,256]{1,0:T(8,128)(2,1)} %k1_hbm.1, bf16[6912,256]{1,0:T(8,128)(2,1)} %kd_hbm.1), custom_call_target="tpu_custom_call" | custom-call | tf_op jit(solution)/shard_map/pallas_call | solution.py:429
  38.6 0.8 %shard_map.68 = (bf16[2,4,16,256]{3,2,1,0:T(8,128)(2,1)}, f32[64,864]{1,0:T(8,128)}, f32[64,864]{1,0:T(8,128)}) custom-call(bf16[2,4,16,256]{3,2,1,0:T(8,128)(2,1)S(1)} %get-tuple-element.9.a_in, f32[64,864]{1,0:T(8,128)S(1)} %get-tuple-element.10.b_in, f32[64,864]{1,0:T(8,128)S(1)} %get-tuple-element.11.c_in), custom_call_target="tpu_custom_call" | custom-call | tf_op jit(solution)/shard_map/pallas_call | solution.py:475
Async XLA Ops:
  0.6 0.8 %copy-start = (bf16[2,4,16,256]{3,2,1,0:T(8,128)(2,1)S(1)}, bf16[2,4,16,256]{3,2,1,0:T(8,128)(2,1)}, u32[]{:S(2)}) copy-start(bf16[2,4,16,256]{3,2,1,0:T(8,128)(2,1)} %clip.1) | copy-start | bytes 196612
  1.5 0.7 %copy-start.1 = (bf16[1,2,8,256]{3,2,1,0:T(8,128)(2,1)S(1)}, bf16[1,2,8,256]{3,2,1,0:T(8,128)(2,1)}, u32[]{:S(2)}) copy-start(bf16[1,2,8,256]{3,2,1,0:T(8,128)(2,1)} %cot.1) | copy-start | bytes 24580

commit v6 on v5

--- a/solution.py
+++ b/solution.py
@@ -236,9 +236,15 @@
         elif d < n_t:
             block_pre(lax.rem(t - d + 2 + n_t, n_t))
 
-    @pl.loop(0, 2)
-    def _(n):
-        block_pre(lax.rem(t + 1 + n, n_t))
+    last = [lax.rem(t + 1 + n, n_t) for n in range(2)]
+    for c in range(3):
+        total = jnp.zeros((576, ch), f32)
+        for a in range(3):
+            for b in range(3):
+                lhs = jnp.concatenate([shifted(2 * s + a, 2, b) for s in last], axis=0)
+                total += dot(lhs, weight(k1, a, b, c))
+        for n, s in enumerate(last):
+            parts[c, pl.ds(2 * s, 2), :, 0:24] = total[288 * n : 288 * n + 288].reshape(2, 6, 24, ch)
 
     row = lax.broadcasted_iota(jnp.int32, (6, 24, ch), 0) + (h * 4 - 1)
     place = lax.broadcasted_iota(jnp.int32, (6, 24, ch), 1)
@@ -384,12 +390,12 @@
     clip_part(0)
     send_all(1)
     clip_part(1)
+    finish(0)
     clip_part(2)
     result = (
         parts[0, 0:2, 0:4, 2:18] + parts[1, 0:2, 0:4, 1:17] + parts[2, 0:2, 0:4, 0:16]
     )
     grad_clip[...] = result.astype(b16)
-    finish(0)
     finish(1)
 
     for d in range(n_t):

time: 39.6 us -> 39.8 us (level)
  no operation moved by 1% of the time
where the time goes in v6:
time: 39.8 us; the launch traced here: 39.6 us
  Pallas kernels  37.5 us (94%)
  local copies, waits for them, and re-layouts  1.53 us (4%)
  between operations  0.65 us (2%)
    pallas_call x1, Pallas kernels, local(): pl.pallas_call(functools.partial(kernel, (n_t, n_h, n_w)), out_shape=[jax...  36.6 us
    unnamed x4, local copies, waits for them, and re-layouts  1.53 us
    pallas_call x1, Pallas kernels, local(): pl.pallas_call(hand_over, out_shape=[jax.ShapeDtypeStruct(x.shape, x.dtyp...  0.82 us

profile of v6, /device:TPU:0, one launch (start us, length us, event | category | flops | bytes accessed | tf_op | source)
XLA Modules:
  0.0 39.6 jit_solution(13422478352056380267)
XLA Ops:
  0.6 0.0 copy-start
  0.6 0.8 %copy-done = bf16[2,4,16,256]{3,2,1,0:T(8,128)(2,1)S(1)} copy-done((bf16[2,4,16,256]{3,2,1,0:T(8,128)(2,1)S(1)}, bf16[2,4,16,256]{3,2,1,0:T(8,128)(2,1)}, u32[]{:S(2)}) %copy-start) | copy-done | bytes 65560
  1.5 0.0 copy-start.1
  1.5 0.7 %copy-done.1 = bf16[1,2,8,256]{3,2,1,0:T(8,128)(2,1)S(1)} copy-done((bf16[1,2,8,256]{3,2,1,0:T(8,128)(2,1)S(1)}, bf16[1,2,8,256]{3,2,1,0:T(8,128)(2,1)}, u32[]{:S(2)}) %copy-start.1) | copy-done | bytes 8216
  2.2 36.6 %shard_map.67 = (bf16[2,4,16,256]{3,2,1,0:T(8,128)(2,1)S(1)}, f32[64,864]{1,0:T(8,128)S(1)}, f32[64,864]{1,0:T(8,128)S(1)}) custom-call(bf16[2,4,16,256]{3,2,1,0:T(8,128)(2,1)S(1)} %copy-done, bf16[1,2,8,256]{3,2,1,0:T(8,128)(2,1)S(1)} %copy-done.1, bf16[6912,256]{1,0:T(8,128)(2,1)} %k1_hbm.1, bf16[6912,256]{1,0:T(8,128)(2,1)} %kd_hbm.1), custom_call_target="tpu_custom_call" | custom-call | tf_op jit(solution)/shard_map/pallas_call | solution.py:435
  38.8 0.8 %shard_map.68 = (bf16[2,4,16,256]{3,2,1,0:T(8,128)(2,1)}, f32[64,864]{1,0:T(8,128)}, f32[64,864]{1,0:T(8,128)}) custom-call(bf16[2,4,16,256]{3,2,1,0:T(8,128)(2,1)S(1)} %get-tuple-element.9.a_in, f32[64,864]{1,0:T(8,128)S(1)} %get-tuple-element.10.b_in, f32[64,864]{1,0:T(8,128)S(1)} %get-tuple-element.11.c_in), custom_call_target="tpu_custom_call" | custom-call | tf_op jit(solution)/shard_map/pallas_call | solution.py:481
Async XLA Ops:
  0.6 0.8 %copy-start = (bf16[2,4,16,256]{3,2,1,0:T(8,128)(2,1)S(1)}, bf16[2,4,16,256]{3,2,1,0:T(8,128)(2,1)}, u32[]{:S(2)}) copy-start(bf16[2,4,16,256]{3,2,1,0:T(8,128)(2,1)} %clip.1) | copy-start | bytes 196612
  1.5 0.7 %copy-start.1 = (bf16[1,2,8,256]{3,2,1,0:T(8,128)(2,1)S(1)}, bf16[1,2,8,256]{3,2,1,0:T(8,128)(2,1)}, u32[]{:S(2)}) copy-start(bf16[1,2,8,256]{3,2,1,0:T(8,128)(2,1)} %cot.1) | copy-start | bytes 24580
